TPU v7x, 128 devices: a whole 4x4x4 slice. The times are simulated.
128 devices in a mesh: seq: 16 (over y, z), head: 8 (over x, core).
Axes of the slice: x: 4, y: 4, z: 4, core: 2. Of those that a mesh axis runs over, the one named last changes fastest.
Arguments:
- block_input: bfloat16 [8192, 2048], P('seq', 'head'), may hold values from -6 to 6
- log_decay: float32 [8192, 16], P('seq', 'head'), may hold values from -2.2 to 0, as said below
- first_gain: float32 [2048], replicated, may hold values from 0.5 to 1.5
- query_weight: bfloat16 [2048, 2048], P(None, 'head'), may hold values from -0.125 to 0.125
- key_weight: bfloat16 [2048, 2048], P(None, 'head'), may hold values from -0.125 to 0.125
- value_weight: bfloat16 [2048, 4096], P(None, 'head'), may hold values from -0.125 to 0.125
- gate_weight: bfloat16 [2048, 4096], P(None, 'head'), may hold values from -0.125 to 0.125
- beta_weight: bfloat16 [2048, 16], P(None, 'head'), may hold values from -0.125 to 0.125
- query_conv: float32 [2048, 4], P('head'), may hold values from -3 to 3
- key_conv: float32 [2048, 4], P('head'), may hold values from -3 to 3
- value_conv: float32 [4096, 4], P('head'), may hold values from -3 to 3
- mixer_gain: float32 [4096], P('head'), may hold values from 0.5 to 1.5
- mixer_weight: bfloat16 [2048, 4096], P(None, 'head'), may hold values from -0.09375 to 0.09375
- second_gain: float32 [2048], replicated, may hold values from 0.5 to 1.5
- swiglu_gate: bfloat16 [2048, 5632], P(None, 'head'), may hold values from -0.125 to 0.125
- swiglu_up: bfloat16 [2048, 5632], P(None, 'head'), may hold values from -0.125 to 0.125
- swiglu_down: bfloat16 [2048, 5632], P(None, 'head'), may hold values from -0.078125 to 0.078125
- cotangent: bfloat16 [8192, 2048], P('seq', 'head'), may hold values from -6 to 6
Outputs:
- output: bfloat16 [8192, 2048], P('seq', 'head')
- grad_input: float32 [8192, 2048], P('seq', 'head')
- grad_first_gain: float32 [2048], P('seq')
- grad_query_weight: float32 [2048, 2048], P('seq', 'head')
- grad_key_weight: float32 [2048, 2048], P('seq', 'head')
- grad_value_weight: float32 [2048, 4096], P('seq', 'head')
- grad_gate_weight: float32 [2048, 4096], P('seq', 'head')
- grad_beta_weight: float32 [2048, 16], P('seq', 'head')
- grad_query_conv: float32 [2048, 4], P('head')
- grad_key_conv: float32 [2048, 4], P('head')
- grad_value_conv: float32 [4096, 4], P('head')
- grad_mixer_gain: float32 [4096], P('head')
- grad_mixer_weight: float32 [2048, 4096], P('seq', 'head')
- grad_second_gain: float32 [2048], P('seq')
- grad_swiglu_gate: float32 [2048, 5632], P('seq', 'head')
- grad_swiglu_up: float32 [2048, 5632], P('seq', 'head')
- grad_swiglu_down: float32 [2048, 5632], P('seq', 'head')
Inputs may be any that keep to these rules, and one draw needn't show every extreme that they name: `log_decay`: every entry is negative.
All inputs are finite; a program needn't handle non-finite values.
Results may differ from a plain program's by a relative error of at most 0.025.
Values may be sent and summed in bfloat16 or wider, within the bound.
No kernel may reach another device: no remote copies, remote signals or barrier semaphores. Data moves between devices by JAX's collectives and lax.ppermute only.
A program may use at most 192 MiB of HBM per device.

v0:
```python
from functools import partial

import jax
import jax.numpy as jnp
from jax import lax
from jax.sharding import Mesh
from jax.sharding import PartitionSpec as P

DK = 128
DV = 256
CH = 64
SEQ = ("seq_0", "seq_1")


HIGH_ACCURACY = lax.Precision.HIGHEST
EPS_NORM = 1e-06
EPS_GATE = 1e-05
FLOAT = jnp.float32
HALF = jnp.bfloat16
CONTRACT_ROWS = (((0,), (0,)), ((), ()))
CONTRACT_COLS = (((1,), (1,)), ((), ()))


def in_order(tiles, dim):
    dims = list(tiles.shape[1:])
    dims[dim] *= tiles.shape[0]
    return jnp.moveaxis(tiles, 0, dim).reshape(dims)


def from_everyone(array, axis):
    size = lax.axis_size(axis)
    return lax.all_to_all(
        jnp.broadcast_to(array[None], (size, *array.shape)), axis, 0, 0, tiled=True
    )


def gathered_copies(array, axis, dim):
    return in_order(from_everyone(array, axis), dim)


def shifted(block, axis, distance):
    devices = range(lax.axis_size(axis))
    route = [(i - distance, i) for i in devices if i - distance in devices]
    return lax.ppermute(block, axis, route)


def filled_with(array, identity):
    return jax.tree.map(
        lambda part, zero: jnp.zeros_like(part) + jnp.asarray(zero, part.dtype), array, identity
    )


def prefix_by_axis(array, axes, combine, identity):
    before = start = filled_with(array, identity)
    total = array
    for axis in reversed(axes):
        size, mine = (lax.axis_size(axis), lax.axis_index(axis))
        pieces = jax.tree.map(lambda part: lax.all_gather(part, axis), total)
        inside, total = (start, start)
        for k in range(size):
            passed = k < mine
            total = combine(total, jax.tree.map(lambda part: part[k], pieces))
            inside = jax.tree.map(lambda new, old: jnp.where(passed, new, old), total, inside)
        before = combine(inside, before)
    return before


def cut_along(array, dim, size):
    before, after = (array.shape[:dim], array.shape[dim + 1 :])
    return jnp.moveaxis(array.reshape(*before, size, -1, *after), dim, 0)


def summed_on_arrival(array, axis, dim):
    tiles = cut_along(array, dim, lax.axis_size(axis))
    arrived = lax.all_to_all(tiles, axis, split_axis=0, concat_axis=0, tiled=True)
    return arrived.astype(jnp.float32).sum(axis=0)


def sent_together(arrays, axis, dim, along):
    columns = [a.reshape(*a.shape[:along], -1) for a in arrays]
    both = jnp.concatenate(columns, axis=along)
    filled, at, done = (lax.psum_scatter(both, axis, scatter_dimension=dim, tiled=True), 0, [])
    for a, column in zip(arrays, columns):
        share = filled[..., at : at + column.shape[along]]
        done.append(share.reshape(*share.shape[:along], *a.shape[along:]))
        at += column.shape[along]
    return tuple(done)


def prefix_by_axis_2(array, axes, combine, identity):
    before = start = filled_with(array, identity)
    total = array
    for axis in reversed(axes):
        size, mine = (lax.axis_size(axis), lax.axis_index(axis))
        pieces = jax.tree.map(
            lambda part, kind: lax.all_gather(part.astype(kind), axis),
            total,
            jax.tree.map(lambda a: jnp.bfloat16 if a.dtype == jnp.float32 else a.dtype, array),
        )
        inside, total = (start, start)
        for k in reversed(range(size)):
            passed = k > mine
            total = combine(
                total, jax.tree.map(lambda part, own: part[k].astype(own.dtype), pieces, array)
            )
            inside = jax.tree.map(lambda new, old: jnp.where(passed, new, old), total, inside)
        before = combine(inside, before)
    return before


def over_copies(array, axis):
    return from_everyone(array, axis).sum(axis=0)


def together(arrays, axis):
    ends = [0]
    for a in arrays:
        ends.append(ends[-1] + a.size)
    total = over_copies(jnp.concatenate([a.ravel() for a in arrays]), axis)
    return tuple((total[b:e].reshape(a.shape) for a, b, e in zip(arrays, ends, ends[1:])))


def rms_norm(values, gain):
    factor = lax.rsqrt(jnp.mean(values * values, axis=-1, keepdims=True) + EPS_NORM)
    return values * factor * gain


def round_keep(values):
    return lax.optimization_barrier(values.astype(HALF)).astype(FLOAT)


def conv_padded(padded, taps):
    length = padded.shape[0] - taps.shape[1] + 1
    summed = padded[0:length] * taps[:, 0]
    for offset in range(1, taps.shape[1]):
        summed = summed + padded[offset : offset + length] * taps[:, offset]
    return summed


def short_convs(pad_query, pad_key, pad_value, taps_query, taps_key, taps_value, head_count):
    queries = jax.nn.silu(conv_padded(pad_query, taps_query))
    raw_keys = jax.nn.silu(conv_padded(pad_key, taps_key))
    tokens = raw_keys.shape[0]
    split_heads = raw_keys.reshape(tokens, head_count, -1)
    key_unit = split_heads * lax.rsqrt(
        jnp.sum(split_heads * split_heads, axis=-1, keepdims=True) + EPS_NORM
    )
    values = jax.nn.silu(conv_padded(pad_value, taps_value))
    return (queries, key_unit.reshape(tokens, -1), values)


def to_blocks(flat_rows, head_count):
    tokens = flat_rows.shape[0]
    return flat_rows.reshape(tokens // CH, CH, head_count, -1).transpose(0, 2, 1, 3)


def group_prep(query_blocks, key_blocks, value_blocks, beta_blocks, decay_blocks):
    gammas = jnp.cumsum(decay_blocks, axis=-1)
    span_len = gammas.shape[-1]
    row_index = lax.broadcasted_iota(jnp.int32, (span_len, span_len), 0)
    col_index = lax.broadcasted_iota(jnp.int32, (span_len, span_len), 1)
    below_mask = row_index > col_index
    within_mask = row_index >= col_index
    spread = gammas[..., :, None] - gammas[..., None, :]
    below_decay = jnp.where(below_mask, jnp.exp(jnp.where(below_mask, spread, 0.0)), 0.0)
    within = jnp.where(within_mask, jnp.exp(jnp.where(within_mask, spread, 0.0)), 0.0)
    key_inner = jnp.einsum("nhik,nhjk->nhij", key_blocks, key_blocks, precision=HIGH_ACCURACY)
    lower_part = beta_blocks[..., :, None] * below_decay * key_inner
    system = jnp.eye(span_len, dtype=FLOAT) + lower_part
    right_side = jnp.concatenate(
        [
            (beta_blocks * jnp.exp(gammas))[..., None] * key_blocks,
            beta_blocks[..., None] * value_blocks,
        ],
        axis=-1,
    )
    solved = jax.scipy.linalg.solve_triangular(system, right_side, lower=True, unit_diagonal=True)
    key_size = key_blocks.shape[-1]
    attention_scores = within * jnp.einsum(
        "nhik,nhjk->nhij", query_blocks, key_blocks, precision=HIGH_ACCURACY
    )
    query_decay_factor = jnp.exp(gammas)[..., None] * query_blocks
    trailing_keys = jnp.exp(gammas[..., -1:] - gammas)[..., None] * key_blocks
    final_block_decay = jnp.exp(gammas[..., -1])
    return (
        query_decay_factor,
        attention_scores,
        solved[..., :key_size],
        solved[..., key_size:],
        trailing_keys,
        final_block_decay,
    )


def group_step(state_sequence, pieces):
    (
        query_decay_factor,
        attention_scores,
        triangular_keys,
        triangular_values,
        trailing_keys,
        final_block_decay,
    ) = pieces
    corrected_values = triangular_values - jnp.einsum(
        "osr,ora->osa", triangular_keys, state_sequence, precision=HIGH_ACCURACY
    )
    output_rows = jnp.einsum(
        "osr,ora->osa", query_decay_factor, state_sequence, precision=HIGH_ACCURACY
    ) + jnp.einsum("wpg,wgt->wpt", attention_scores, corrected_values, precision=HIGH_ACCURACY)
    following_states = final_block_decay[:, None, None] * state_sequence + jnp.einsum(
        "fnb,fnx->fbx", trailing_keys, corrected_values, precision=HIGH_ACCURACY
    )
    return (following_states, output_rows)


def affine_step(carried, pieces):
    mapping, state_sequence = carried
    (
        query_decay_factor,
        attention_scores,
        triangular_keys,
        triangular_values,
        trailing_keys,
        final_block_decay,
    ) = pieces
    eye_mat = jnp.eye(triangular_keys.shape[-1], dtype=FLOAT)
    step_matrix = final_block_decay[:, None, None] * eye_mat - jnp.einsum(
        "hck,hcl->hkl", trailing_keys, triangular_keys, precision=HIGH_ACCURACY
    )
    mapping_next = jnp.einsum("hij,hjk->hik", step_matrix, mapping, precision=HIGH_ACCURACY)
    following_states = jnp.einsum(
        "wpg,wgt->wpt", step_matrix, state_sequence, precision=HIGH_ACCURACY
    ) + jnp.einsum("fnb,fnx->fbx", trailing_keys, triangular_values, precision=HIGH_ACCURACY)
    return ((mapping_next, following_states), None)


def compose(earlier, later_part):
    return (
        jnp.einsum("hij,hjk->hik", later_part[0], earlier[0], precision=HIGH_ACCURACY),
        jnp.einsum("wpg,wgt->wpt", later_part[0], earlier[1], precision=HIGH_ACCURACY)
        + later_part[1],
    )


def mixer_local(query_in, key_in, value_in, beta_in, initial, decay_blocks, head_count):
    beta_blocks = beta_in.reshape(-1, CH, head_count).transpose(0, 2, 1)
    pieces = group_prep(
        to_blocks(query_in, head_count),
        to_blocks(key_in, head_count),
        to_blocks(value_in, head_count),
        beta_blocks,
        decay_blocks,
    )
    final_state, output_rows = lax.scan(group_step, initial, pieces)
    return (
        output_rows.transpose(0, 2, 1, 3).reshape(-1, head_count, output_rows.shape[-1]),
        final_state,
    )


def gate_norm(mixed_out, gate_pre, mixer_gain):
    tokens = mixed_out.shape[0]
    factor = lax.rsqrt(jnp.mean(mixed_out * mixed_out, axis=-1, keepdims=True) + EPS_GATE)
    scaled = (mixed_out * factor).reshape(tokens, -1)
    return scaled * mixer_gain * jax.nn.silu(gate_pre)


def swiglu(gate_act, up_act):
    return jax.nn.silu(gate_act) * up_act


def shards(
    block_input,
    log_decay,
    first_gain,
    query_weight,
    key_weight,
    value_weight,
    gate_weight,
    beta_weight,
    query_conv,
    key_conv,
    value_conv,
    mixer_gain,
    mixer_weight,
    second_gain,
    swiglu_gate,
    swiglu_up,
    swiglu_down,
    cotangent,
):
    head_count = log_decay.shape[1]
    tokens = block_input.shape[0]
    rim_rows = query_conv.shape[1] - 1
    slice_width = block_input.shape[1]
    column_start = lax.axis_index("head") * slice_width
    query_cols = query_weight.shape[1]
    key_cols = key_weight.shape[1]
    whole_input = gathered_copies(block_input, "head", 1).astype(FLOAT)
    first_normed, first_back = jax.vjp(rms_norm, whole_input, first_gain)
    first_normed = first_normed.astype(HALF)
    proj_query = jnp.dot(first_normed, query_weight, preferred_element_type=FLOAT).astype(HALF)
    proj_key = jnp.dot(first_normed, key_weight, preferred_element_type=FLOAT).astype(HALF)
    proj_value = jnp.dot(first_normed, value_weight, preferred_element_type=FLOAT).astype(HALF)
    gate_pre = jnp.dot(first_normed, gate_weight, preferred_element_type=FLOAT)
    beta_vals = jax.nn.sigmoid(jnp.dot(first_normed, beta_weight, preferred_element_type=FLOAT))
    stacked = jnp.concatenate([proj_query, proj_key, proj_value], axis=1)
    carried = shifted(stacked[tokens - rim_rows :], SEQ, 1)
    padded = jnp.concatenate([carried, stacked], axis=0).astype(FLOAT)
    conv_out, conv_back = jax.vjp(
        partial(short_convs, head_count=head_count),
        padded[:, :query_cols],
        padded[:, query_cols : query_cols + key_cols],
        padded[:, query_cols + key_cols :],
        query_conv,
        key_conv,
        value_conv,
    )
    queries = round_keep(conv_out[0])
    key_unit = round_keep(conv_out[1])
    values = round_keep(conv_out[2])
    decay_blocks = log_decay.reshape(-1, CH, head_count).transpose(0, 2, 1)
    beta_blocks = beta_vals.reshape(-1, CH, head_count).transpose(0, 2, 1)
    pieces = group_prep(
        to_blocks(queries, head_count),
        to_blocks(key_unit, head_count),
        to_blocks(values, head_count),
        beta_blocks,
        decay_blocks,
    )
    eye_stack = jnp.broadcast_to(jnp.eye(DK, dtype=FLOAT), (head_count, DK, DK))
    zero_state = jnp.zeros((head_count, DK, DV), FLOAT)
    (mapping, local_end), ignored = lax.scan(affine_step, (eye_stack, zero_state), pieces)
    identity = (eye_stack, zero_state)
    prior_map, initial = prefix_by_axis((mapping, local_end), SEQ, compose, identity)
    mixer_fn = partial(mixer_local, decay_blocks=decay_blocks, head_count=head_count)
    (mixed_out, final_state), mixer_back = jax.vjp(
        mixer_fn, queries, key_unit, values, beta_vals, initial
    )
    gated_out, gate_back = jax.vjp(gate_norm, mixed_out, gate_pre, mixer_gain)
    gated_out = gated_out.astype(HALF)
    branch_part = lax.dot_general(
        gated_out, mixer_weight, CONTRACT_COLS, preferred_element_type=FLOAT
    )
    branch = lax.psum(branch_part, "head")
    hidden = whole_input + branch
    second_normed, second_back = jax.vjp(rms_norm, hidden, second_gain)
    second_normed = second_normed.astype(HALF)
    gate_act = jnp.dot(second_normed, swiglu_gate, preferred_element_type=FLOAT)
    up_act = jnp.dot(second_normed, swiglu_up, preferred_element_type=FLOAT)
    product, swiglu_back = jax.vjp(swiglu, gate_act, up_act)
    product = product.astype(HALF)
    down_part = lax.dot_general(product, swiglu_down, CONTRACT_COLS, preferred_element_type=FLOAT)
    down_mine = summed_on_arrival(down_part.astype(jnp.bfloat16), "head", 1)
    hidden_mine = lax.dynamic_slice_in_dim(hidden, column_start, slice_width, 1)
    output = (hidden_mine + down_mine).astype(HALF)
    whole_cot = gathered_copies(cotangent, "head", 1)
    grad_swiglu_down = lax.dot_general(
        whole_cot, product, CONTRACT_ROWS, preferred_element_type=FLOAT
    )
    d_product = jnp.dot(whole_cot, swiglu_down, preferred_element_type=FLOAT)
    d_gate, d_up = swiglu_back(d_product)
    d_gate = d_gate.astype(HALF)
    d_up = d_up.astype(HALF)
    grad_swiglu_gate = lax.dot_general(
        second_normed, d_gate, CONTRACT_ROWS, preferred_element_type=FLOAT
    )
    grad_swiglu_up = lax.dot_general(
        second_normed, d_up, CONTRACT_ROWS, preferred_element_type=FLOAT
    )
    d_second_part = lax.dot_general(
        d_gate, swiglu_gate, CONTRACT_COLS, preferred_element_type=FLOAT
    ) + lax.dot_general(d_up, swiglu_up, CONTRACT_COLS, preferred_element_type=FLOAT)
    d_second = lax.psum(d_second_part.astype(jnp.bfloat16), "head").astype(jnp.float32)
    d_hidden_norm, grad_second_gain = second_back(d_second)
    d_hidden = whole_cot.astype(FLOAT) + d_hidden_norm
    d_hidden_mine = lax.dynamic_slice_in_dim(d_hidden, column_start, slice_width, 1)
    d_branch = d_hidden.astype(HALF)
    grad_swiglu_gate, grad_swiglu_up, grad_swiglu_down, grad_second_gain = tuple(
        (
            part.astype(jnp.float32)
            for part in sent_together(
                (
                    grad_swiglu_gate.astype(jnp.bfloat16),
                    grad_swiglu_up.astype(jnp.bfloat16),
                    grad_swiglu_down.astype(jnp.bfloat16),
                    grad_second_gain.astype(jnp.bfloat16),
                ),
                SEQ,
                0,
                1,
            )
        )
    )
    grad_mixer_weight = lax.dot_general(
        d_branch, gated_out, CONTRACT_ROWS, preferred_element_type=FLOAT
    )
    d_gated = jnp.dot(d_branch, mixer_weight, preferred_element_type=FLOAT)
    d_mixed, d_gate_pre, grad_mixer_gain = gate_back(d_gated)
    d_gate_pre = d_gate_pre.astype(HALF)
    local_grads = mixer_back((d_mixed, jnp.zeros_like(final_state)))
    reverse_map = jnp.swapaxes(mapping, 1, 2)
    later_map, d_end = prefix_by_axis_2((reverse_map, local_grads[4]), SEQ, compose, identity)
    carried_grads = mixer_back((jnp.zeros_like(mixed_out), d_end))
    d_queries = local_grads[0] + carried_grads[0]
    d_keys = local_grads[1] + carried_grads[1]
    d_values = local_grads[2] + carried_grads[2]
    d_betas = local_grads[3] + carried_grads[3]
    conv_grads = conv_back((d_queries, d_keys, d_values))
    grad_query_conv = conv_grads[3]
    grad_key_conv = conv_grads[4]
    grad_value_conv = conv_grads[5]
    d_padded = jnp.concatenate([conv_grads[0], conv_grads[1], conv_grads[2]], axis=1)
    incoming = shifted(d_padded[:rim_rows], SEQ, -1)
    d_stacked = jnp.concatenate(
        [d_padded[rim_rows:tokens], d_padded[tokens:] + incoming], axis=0
    ).astype(HALF)
    d_proj_query = d_stacked[:, :query_cols]
    d_proj_key = d_stacked[:, query_cols : query_cols + key_cols]
    d_proj_value = d_stacked[:, query_cols + key_cols :]
    d_beta_logit = d_betas * beta_vals * (1.0 - beta_vals)
    grad_query_weight = lax.dot_general(
        first_normed, d_proj_query, CONTRACT_ROWS, preferred_element_type=FLOAT
    )
    grad_key_weight = lax.dot_general(
        first_normed, d_proj_key, CONTRACT_ROWS, preferred_element_type=FLOAT
    )
    grad_value_weight = lax.dot_general(
        first_normed, d_proj_value, CONTRACT_ROWS, preferred_element_type=FLOAT
    )
    grad_gate_weight = lax.dot_general(
        first_normed, d_gate_pre, CONTRACT_ROWS, preferred_element_type=FLOAT
    )
    grad_beta_weight = jnp.einsum(
        "td,th->dh", first_normed, d_beta_logit, preferred_element_type=FLOAT
    )
    d_first_part = lax.dot_general(
        d_proj_query, query_weight, CONTRACT_COLS, preferred_element_type=FLOAT
    )
    d_first_part = d_first_part + lax.dot_general(
        d_proj_key, key_weight, CONTRACT_COLS, preferred_element_type=FLOAT
    )
    d_first_part = d_first_part + lax.dot_general(
        d_proj_value, value_weight, CONTRACT_COLS, preferred_element_type=FLOAT
    )
    d_first_part = d_first_part + lax.dot_general(
        d_gate_pre, gate_weight, CONTRACT_COLS, preferred_element_type=FLOAT
    )
    d_first_part = d_first_part + jnp.einsum(
        "th,dh->td", d_beta_logit, beta_weight, preferred_element_type=FLOAT
    )
    d_first = lax.psum(d_first_part.astype(jnp.bfloat16), "head").astype(jnp.float32)
    d_input_norm, grad_first_gain = first_back(d_first)
    grad_input = d_hidden_mine + lax.dynamic_slice_in_dim(
        d_input_norm, column_start, slice_width, 1
    )
    grad_query_conv, grad_key_conv, grad_value_conv, grad_mixer_gain = together(
        (grad_query_conv, grad_key_conv, grad_value_conv, grad_mixer_gain), SEQ
    )
    (
        grad_query_weight,
        grad_key_weight,
        grad_value_weight,
        grad_gate_weight,
        grad_beta_weight,
        grad_mixer_weight,
        grad_first_gain,
    ) = tuple(
        (
            part.astype(jnp.float32)
            for part in sent_together(
                (
                    grad_query_weight.astype(jnp.bfloat16),
                    grad_key_weight.astype(jnp.bfloat16),
                    grad_value_weight.astype(jnp.bfloat16),
                    grad_gate_weight.astype(jnp.bfloat16),
                    grad_beta_weight.astype(jnp.bfloat16),
                    grad_mixer_weight.astype(jnp.bfloat16),
                    grad_first_gain.astype(jnp.bfloat16),
                ),
                SEQ,
                0,
                1,
            )
        )
    )
    return (
        output,
        grad_input,
        grad_first_gain,
        grad_query_weight,
        grad_key_weight,
        grad_value_weight,
        grad_gate_weight,
        grad_beta_weight,
        grad_query_conv,
        grad_key_conv,
        grad_value_conv,
        grad_mixer_gain,
        grad_mixer_weight,
        grad_second_gain,
        grad_swiglu_gate,
        grad_swiglu_up,
        grad_swiglu_down,
    )


def solution(mesh):
    torus = Mesh(mesh.devices.reshape(4, 4, mesh.shape["head"]), ("seq_0", "seq_1", "head"))
    in_specs = (
        P(SEQ, "head"),
        P(SEQ, "head"),
        P(),
        P(None, "head"),
        P(None, "head"),
        P(None, "head"),
        P(None, "head"),
        P(None, "head"),
        P("head", None),
        P("head", None),
        P("head", None),
        P("head"),
        P(None, "head"),
        P(),
        P(None, "head"),
        P(None, "head"),
        P(None, "head"),
        P(SEQ, "head"),
    )
    out_specs = (
        P(SEQ, "head"),
        P(SEQ, "head"),
        P(SEQ),
        P(SEQ, "head"),
        P(SEQ, "head"),
        P(SEQ, "head"),
        P(SEQ, "head"),
        P(SEQ, "head"),
        P("head", None),
        P("head", None),
        P("head", None),
        P("head"),
        P(SEQ, "head"),
        P(SEQ),
        P(SEQ, "head"),
        P(SEQ, "head"),
        P(SEQ, "head"),
    )
    return jax.shard_map(
        shards, mesh=torus, in_specs=in_specs, out_specs=out_specs, check_vma=False
    )
```

profile of v0, /device:TPU:2, one launch (start us, length us, event | category | flops | bytes accessed | tf_op | source)
XLA Modules:
  0.0 1168.7 jit_solution(14016950947746270802)
XLA Ops:
  9.8 5.0 all-to-all-start
  18.7 21.9 %all-to-all-done = bf16[8,512,256]{2,1,0:T(8,128)(2,1)} async-done(((bf16[8,512,256]{2,1,0:T(8,128)(2,1)}), bf16[8,512,256]{2,1,0:T(8,128)(2,1)}, u32[]{:S(2)}, u32[]{:S(2)}) %all-to-all-start) | async-done | bytes 2097184 | tf_op jit(solution)/shard_map/all_to_all | solution.py:32
  53.9 4.8 collective-permute-start
  71.2 5.4 multiply_convert_fusion.5
  86.6 80.0 %custom-call.11 = f32[8,2,1,64,64]{3,4,2,1,0:T(8,128)} custom-call(f32[8,2,1,64,64]{4,3,2,1,0:T(8,128)} %fusion.171), custom_call_target="InvertDiagBlocksLowerTriangular" | custom-call | tf_op jit(solution)/shard_map/jit(_solve_triangular)/vmap(vmap())/triangular_solve/custom-call.1 | solution.py:177
  173.1 44.6 %while.82 = (s32[]{:T(128)}, f32[2,128,128]{2,1,0:T(8,128)S(1)}, f32[2,128,256]{2,1,0:T(8,128)}, f32[8,2]{1,0:T(8,128)}, f32[8,2,64,128]{3,2,1,0:T(8,128)}, /*in...) while((s32[]{:T(128)}, f32[2,128,128]{2,1,0:T(8,128)S(1)}, ...), condition=%wide.region_4.6_spmd.clone, body=%wide.region_3.5_spmd.clone.sunk | while | flops 226721792 | bytes 2427019 | solution.py:333
  220.2 5.8 all-to-all-start.2
  230.2 17.3 %all-gather = f32[8,128,128]{2,1,0:T(8,128)S(1)} all-gather(f32[2,128,128]{2,1,0:T(8,128)S(1)} %get-tuple-element.701), channel_id=2, replica_groups=mesh['seq_0'=4,'seq_1'=4,'head'=8] {'seq_1'}, dimensions={0}, use_global_device_ids=true | all-gather | bytes 655360 | tf_op jit(solution)/shard_map/all_gather | solution.py:58
  258.6 16.4 %all-gather.1 = f32[8,128,128]{2,1,0:T(8,128)} all-gather(f32[2,128,128]{2,1,0:T(8,128)S(1)} %fusion.351), channel_id=3, replica_groups=mesh['seq_0'=4,'seq_1'=4,'head'=8] {'seq_0'}, dimensions={0}, use_global_device_ids=true | all-gather | bytes 655360 | tf_op jit(solution)/shard_map/all_gather | solution.py:58
  286.2 69.9 %while.80 = (s32[]{:T(128)}, f32[2,128,256]{2,1,0:T(8,128)S(1)}, f32[8,2,64,256]{3,1,2,0:T(2,128)}, f32[8,2,128,256]{3,2,1,0:T(8,128)}, f32[8,2,64,256]{3,2,1,0:...) while((s32[]{:T(128)}, f32[2,128,256]{2,1,0:T(8,128)S(1)}, ...), condition=%wide.region_6.8_spmd, body=%wide.region_5.7_spmd.sunk | while | flops 176357376 | bytes 3147961 | solution.py:254
  364.3 5.0 multiply_convert_fusion.4
  381.6 12.7 %all-gather.4 = bf16[8,128,128]{2,1,0:T(8,128)(2,1)S(1)} all-gather(bf16[2,128,128]{2,1,0:T(8,128)(2,1)S(1)} %bitcast.559), channel_id=6, replica_groups=mesh['seq_0'=4,'seq_1'=4,'head'=8] {'seq_1'}, dimensions={0}, use_global_device_ids=true | all-gather | bytes 327680 | tf_op jit(solution)/shard_map/all_gather | solution.py:96
  395.2 13.4 %all-gather.5 = bf16[8,128,128]{2,1,0:T(8,128)(2,1)} all-gather(bf16[2,128,128]{2,1,0:T(8,128)(2,1)S(1)} %get-tuple-element.1376), channel_id=7, replica_groups=mesh['seq_0'=4,'seq_1'=4,'head'=8] {'seq_0'}, dimensions={0}, use_global_device_ids=true | all-gather | bytes 327680 | tf_op jit(solution)/shard_map/all_gather | solution.py:96
  411.1 32.9 %all-reduce.32.cloned.1.call-done = f32[512,2048]{1,0:T(8,128)} async-done(((f32[512,2048]{1,0:T(8,128)}), f32[512,2048]{1,0:T(8,128)}) %all-reduce.32.cloned.1.call-update) | async-done | bytes 4194320 | tf_op jit(solution)/shard_map/psum | solution.py:345
  464.3 5.3 convolution_convert_fusion
  476.1 54.0 %all-reduce.34.cloned.1.call-done = bf16[512,2048]{1,0:T(8,128)(2,1)} async-done(((bf16[512,2048]{1,0:T(8,128)(2,1)}), bf16[512,2048]{1,0:T(8,128)(2,1)}) %all-reduce.34.cloned.1.call-update) | async-done | bytes 2097168 | tf_op jit(solution)/shard_map/psum | solution.py:374
  559.3 116.9 %while.83 = (s32[]{:T(128)}, f32[2,128,256]{2,1,0:T(8,128)S(1)}, f32[8,2,64,128]{3,2,1,0:T(8,128)}, f32[8,2,64,64]{3,2,1,0:T(8,128)}, f32[8,2,64,128]{3,2,1,0:T(...) while((s32[]{:T(128)}, f32[2,128,256]{2,1,0:T(8,128)S(1)}, ...), condition=%wide.region_15.17_spmd.clone, body=%wide.region_14.16_spmd.clone.sunk | while | flops 352813056 | bytes 4462320 | solution.py:254
  683.6 14.1 %all-gather.6 = bf16[8,128,256]{2,1,0:T(8,128)(2,1)S(1)} all-gather(bf16[2,128,256]{2,1,0:T(8,128)(2,1)S(1)} %convert_element_type.315), channel_id=8, replica_groups=mesh['seq_0'=4,'seq_1'=4,'head'=8] {'seq_1'}, dimensions={0}, use_global_device_ids=true | all-gather | bytes 655360 | tf_op jit(solution)/shard_map/all_gather | solution.py:96
  698.8 13.3 %all-gather.7 = bf16[8,128,256]{2,1,0:T(8,128)(2,1)S(1)} all-gather(bf16[2,128,256]{2,1,0:T(8,128)(2,1)S(1)} %get-tuple-element.1378), channel_id=9, replica_groups=mesh['seq_0'=4,'seq_1'=4,'head'=8] {'seq_0'}, dimensions={0}, use_global_device_ids=true | all-gather | bytes 655360 | tf_op jit(solution)/shard_map/all_gather | solution.py:96
  718.6 108.8 %while.81 = (s32[]{:T(128)}, f32[2,128,256]{2,1,0:T(8,128)S(1)}, f32[8,2,64,128]{3,2,1,0:T(8,128)}, f32[8,2,64,64]{3,2,1,0:T(8,128)}, f32[8,2,64,128]{3,2,1,0:T(...) while((s32[]{:T(128)}, f32[2,128,256]{2,1,0:T(8,128)S(1)}, ...), condition=%wide.region_17.19_spmd, body=%wide.region_16.18_spmd.sunk | while | flops 352616448 | bytes 3675345 | solution.py:254
  858.6 4.9 multiply_reduce_fusion.6
  888.5 8.7 collective-permute-done.1
  905.2 7.2 pad_maximum_fusion
  912.4 11.8 %copy.464 = bf16[2048,2113]{1,0:T(8,128)(2,1)} copy(bf16[2048,2113]{0,1:T(8,128)(2,1)} %pad_maximum_fusion) | data formatting | bytes 17309696
  938.1 33.8 %all-reduce.36.cloned.1.call-done = bf16[512,2048]{1,0:T(8,128)(2,1)} async-done(((bf16[512,2048]{1,0:T(8,128)(2,1)}), bf16[512,2048]{1,0:T(8,128)(2,1)}) %all-reduce.36.cloned.1.call-update) | async-done | bytes 2097168 | tf_op jit(solution)/shard_map/psum | solution.py:452
  971.9 6.1 fusion.116
  978.0 43.3 %concatenate.31 = bf16[2048,2051]{0,1:T(8,128)(2,1)} concatenate(bf16[2048,256]{0,1:T(8,128)(2,1)} %convolution_convert_fusion.8, bf16[2048,256]{0,1:T(8,128)(2,1)} %convolution_convert_fusion.7, bf16[2048,512]{0,1:T(8,128)(2,1)} %convolution_convert_fusion.5, bf16[2048,512]{0,1:T(8,128)(2,1)} %convolution_convert_fusion.4, bf16[2048,2]{0,1:T(2,128)(2,1)S(1)} %convolution_convert_fusion.9, ...), dimensions={1} | concatenate | bytes 16801792 | tf_op jit(solution)/shard_map/concatenate | solution.py:81
  1021.4 11.7 copy.462
  1034.8 7.2 all-to-all-start.3
  1050.7 7.3 all-to-all-start.1
  1061.3 22.5 %all-to-all-done.1 = bf16[8,512,256]{2,1,0:T(8,128)(2,1)} async-done(((bf16[8,512,256]{2,1,0:T(8,128)(2,1)}), bf16[8,512,256]{2,1,0:T(8,128)(2,1)}, u32[]{:S(2)}, u32[]{:S(2)}) %all-to-all-start.1) | async-done | bytes 2097184 | tf_op jit(solution)/shard_map/all_to_all | solution.py:75
  1097.2 55.7 %reduce-scatter.7.cloned.1.call-done = bf16[128,2051]{1,0:T(8,128)(2,1)} async-done(((bf16[2048,2051]{1,0:T(8,128)(2,1)}), bf16[128,2051]{1,0:T(8,128)(2,1)}) %reduce-scatter.7.cloned.1.call-update) | async-done | bytes 525072
  (866 shorter events, 623.8 us)
Async XLA Ops:
  7.2 448.5 %copy-start = (bf16[2048,704]{0,1:T(8,128)(2,1)S(1)}, bf16[2048,704]{0,1:T(8,128)(2,1)}, u32[]{:S(2)}) copy-start(bf16[2048,704]{0,1:T(8,128)(2,1)} %param.48) | copy-start | bytes 8650756
  9.8 30.8 %all-to-all-start = ((bf16[8,512,256]{2,1,0:T(8,128)(2,1)}), bf16[8,512,256]{2,1,0:T(8,128)(2,1)}, u32[]{:S(2)}, u32[]{:S(2)}) async-start(bf16[8,512,256]{2,1,0:T(8,128)(2,1)} %broadcast_in_dim.253), calls=%async_computation | async-start | bytes 4194304 | tf_op jit(solution)/shard_map/all_to_all | solution.py:32
  14.8 233.8 %all-gather.11.cloned.1.call-start = ((), (), s32[]{:S(2)}) async-start(), calls=%async_computation.9 | async-start | bytes 1310720 | tf_op jit(solution)/shard_map/all_gather | solution.py:58
  15.3 44.2 %copy-start.100 = (f32[8,2,64]{2,0,1:T(8,128)}, f32[8,2,64]{2,0,1:T(8,128)S(1)}, u32[]{:S(2)}) copy-start(f32[8,2,64]{2,0,1:T(8,128)S(1)} %reduce_window_sum.12) | copy-start | bytes 12292
  16.2 156.9 %copy-start.33 = (f32[128,128]{1,0:T(8,128)}, f32[128,128]{1,0:T(8,128)S(1)}, u32[]{:S(2)}) copy-start(f32[128,128]{1,0:T(8,128)S(1)} %fusion.290) | copy-start | bytes 196612
  18.7 66.8 %copy-start.95 = (pred[64,64]{1,0:T(8,128)(4,1)}, pred[64,64]{1,0:T(8,128)(4,1)S(1)}, u32[]{:S(2)}) copy-start(pred[64,64]{1,0:T(8,128)(4,1)S(1)} %get-tuple-element.1382) | copy-start | bytes 12292
  18.7 66.8 %copy-start.102 = (pred[64,64]{1,0:T(8,128)(4,1)}, pred[64,64]{1,0:T(8,128)(4,1)S(1)}, u32[]{:S(2)}) copy-start(pred[64,64]{1,0:T(8,128)(4,1)S(1)} %get-tuple-element.1381) | copy-start | bytes 12292
  53.9 9.5 collective-permute-start
  60.2 106.5 %copy-start.107 = (f32[8,2,64]{2,1,0:T(2,128)}, f32[8,2,64]{2,1,0:T(2,128)S(1)}, u32[]{:S(2)}) copy-start(f32[8,2,64]{2,1,0:T(2,128)S(1)} %copy.372) | copy-start | bytes 12292
  60.2 106.4 %copy-start.109 = (f32[8,2,64]{2,1,0:T(2,128)}, f32[8,2,64]{2,1,0:T(2,128)S(1)}, u32[]{:S(2)}) copy-start(f32[8,2,64]{2,1,0:T(2,128)S(1)} %copy.364) | copy-start | bytes 12292
  220.2 153.4 %all-to-all-start.2 = ((bf16[8,512,256]{2,1,0:T(8,128)(2,1)}), bf16[8,512,256]{2,1,0:T(8,128)(2,1)}, u32[]{:S(2)}, u32[]{:S(2)}) async-start(bf16[8,512,256]{2,1,0:T(8,128)(2,1)} %broadcast_in_dim.259), calls=%async_computation.2 | async-start | bytes 4194304 | tf_op jit(solution)/shard_map/all_to_all | solution.py:32
  226.0 22.2 %copy-start.34 = (f32[128,128]{1,0:T(8,128)S(1)}, f32[128,128]{1,0:T(8,128)}, u32[]{:S(2)}) copy-start(f32[128,128]{1,0:T(8,128)} %copy-done.33) | copy-start | bytes 196612
  226.0 54.5 %all-gather.13.cloned.1.call-start = ((), (), s32[]{:S(2)}) async-start(), calls=%async_computation.10 | async-start | bytes 1310720 | tf_op jit(solution)/shard_map/all_gather | solution.py:58
  226.1 50.9 %copy-start.98 = (pred[64,64]{1,0:T(8,128)(4,1)}, pred[64,64]{1,0:T(8,128)(4,1)S(1)}, u32[]{:S(2)}) copy-start(pred[64,64]{1,0:T(8,128)(4,1)S(1)} %iota_compare_fusion.4) | copy-start | bytes 12292
  226.1 49.8 %copy-start.104 = (f32[8,2,64]{2,1,0:T(2,128)}, f32[8,2,64]{2,1,0:T(2,128)S(1)}, u32[]{:S(2)}) copy-start(f32[8,2,64]{2,1,0:T(2,128)S(1)} %copy.378) | copy-start | bytes 12292
  255.0 189.0 %all-reduce.32.cloned.1.call-start = ((), (), s32[]{:S(2)}) async-start(), calls=%async_computation.6 | async-start | bytes 8388608 | tf_op jit(solution)/shard_map/psum | solution.py:345
  255.0 20.9 %copy-start.47 = (bf16[8,64,2,128]{3,1,2,0:T(8,128)(2,1)S(1)}, bf16[8,64,2,128]{3,1,2,0:T(8,128)(2,1)}, u32[]{:S(2)}) copy-start(bf16[8,64,2,128]{3,1,2,0:T(8,128)(2,1)} %copy.380) | copy-start | bytes 786436
  373.5 156.5 %all-reduce.34.cloned.1.call-start = ((), (), s32[]{:S(2)}) async-start(), calls=%async_computation.7 | async-start | bytes 4194304 | tf_op jit(solution)/shard_map/psum | solution.py:374
  377.5 16.8 %copy-start.36 = (f32[128,128]{1,0:T(8,128)S(1)}, f32[128,128]{1,0:T(8,128)}, u32[]{:S(2)}) copy-start(f32[128,128]{1,0:T(8,128)} %copy-done.33) | copy-start | bytes 196612
  411.1 36.9 %copy-start.111 = (f32[2048]{0:T(1024)S(1)}, f32[2048]{0:T(1024)}, u32[]{:S(2)}) copy-start(f32[2048]{0:T(1024)} %param.45) | copy-start | bytes 24580
  464.0 507.9 %all-reduce.36.cloned.1.call-start = ((), (), s32[]{:S(2)}) async-start(), calls=%async_computation.8 | async-start | bytes 4194304 | tf_op jit(solution)/shard_map/psum | solution.py:452
  681.0 16.7 %copy-start.22 = (bf16[8,128,128]{2,1,0:T(8,128)(2,1)S(1)}, bf16[8,128,128]{2,1,0:T(8,128)(2,1)}, u32[]{:S(2)}) copy-start(bf16[8,128,128]{2,1,0:T(8,128)(2,1)} %copy-done.21) | copy-start | bytes 786436
  683.6 28.4 %copy-start.58 = (bf16[8,128,128]{2,1,0:T(8,128)(2,1)S(1)}, bf16[8,128,128]{2,1,0:T(8,128)(2,1)}, u32[]{:S(2)}) copy-start(bf16[8,128,128]{2,1,0:T(8,128)(2,1)} %all-gather.5) | copy-start | bytes 786436
  698.8 14.4 %copy-start.93 = (f32[2,128,128]{2,1,0:T(8,128)S(1)}, f32[2,128,128]{2,1,0:T(8,128)}, u32[]{:S(2)}) copy-start(f32[2,128,128]{2,1,0:T(8,128)} %fusion.258) | copy-start | bytes 393220
  886.1 11.1 collective-permute-start.1
  905.1 184.9 %reduce-scatter.9.cloned.1.call-start = ((), (), s32[]{:S(2)}) async-start(), calls=%async_computation.12 | async-start | bytes 9469952
  924.2 228.6 %reduce-scatter.7.cloned.1.call-start = ((), (), s32[]{:S(2)}) async-start(), calls=%async_computation.11 | async-start | bytes 9469952
  935.4 36.5 %copy-start.126 = (f32[2048]{0:T(1024)S(1)}, f32[2048]{0:T(1024)}, u32[]{:S(2)}) copy-start(f32[2048]{0:T(1024)} %param.34) | copy-start | bytes 24580
  935.4 36.5 %copy-start.128 = (f32[512]{0:T(512)S(1)}, f32[512]{0:T(512)}, u32[]{:S(2)}) copy-start(f32[512]{0:T(512)} %copy-done.127) | copy-start | bytes 6148
  1034.8 15.8 %all-to-all-start.3 = ((f32[16,1,4608]{2,1,0:T(1,128)}), f32[16,1,4608]{2,1,0:T(1,128)S(1)}, u32[]{:S(2)}, u32[]{:S(2)}) async-start(f32[16,1,4608]{2,1,0:T(1,128)} %broadcast_in_dim.278), calls=%async_computation.3 | async-start | bytes 589824 | tf_op jit(solution)/shard_map/all_to_all | solution.py:32
  1050.7 33.1 %all-to-all-start.1 = ((bf16[8,512,256]{2,1,0:T(8,128)(2,1)}), bf16[8,512,256]{2,1,0:T(8,128)(2,1)}, u32[]{:S(2)}, u32[]{:S(2)}) async-start(bf16[8,512,256]{2,1,0:T(8,128)(2,1)} %bitcast.555), calls=%async_computation.1 | async-start | bytes 4194304 | tf_op jit(solution)/shard_map/all_to_all | solution.py:75
  1060.6 27.0 %copy-start.139 = (f32[512]{0:T(512)S(1)}, f32[512]{0:T(512)}, u32[]{:S(2)}) copy-start(f32[512]{0:T(512)} %copy-done.138) | copy-start | bytes 6148
  (148 other events, 489.1 us)
Sparse Core Ops, SparseCore 0:
  217.8 28.0 all-gather.10
  255.1 25.3 all-gather.12
  373.6 70.2 all-reduce.31
  464.2 65.8 all-reduce.33
  905.3 66.5 all-reduce.35
  975.2 88.2 reduce-scatter.8
  1067.3 85.4 reduce-scatter.6
where the time goes:
time: 1180 us; the launch traced here: 1170 us
  matrix products  398 us (34%)
  waiting for transfers between devices  239 us (20%)
  local copies, waits for them, and re-layouts  227 us (19%)
  other arithmetic  168 us (14%)
  blocking collectives  87 us (7%)
  starting transfers between devices  32.2 us (3%)
  between operations  16.6 us (1%)
    another operation x4, other arithmetic, group_prep(): jax.scipy.linalg.solve_triangular(system, right_side, lower=True, unit_di...  81.2 us
    dot_general x40, matrix products, group_step(): jnp.einsum('osr,ora->osa', triangular_keys, state_sequence, precision=HIG...  66.5 us
    dot_general x40, matrix products, group_step(): jnp.einsum('wpg,wgt->wpt', attention_scores, corrected_values, precision=...  64.7 us
    dot_general x40, matrix products, group_step(): jnp.einsum('osr,ora->osa', query_decay_factor, state_sequence, precision=...  60.2 us
    dot_general x40, matrix products, group_step(): jnp.einsum('fnb,fnx->fbx', trailing_keys, corrected_values, precision=HIG...  58.6 us
    unnamed x356, local copies, waits for them, and re-layouts  56.1 us
    unnamed x9, waiting for transfers between devices  55.8 us
    psum x1, waiting for transfers between devices, shards(): lax.psum(d_second_part.astype(jnp.bfloat16), 'head').astype(jnp.float32)  54 us
  transfers between devices with their start and end apart: 13, of which 10 were waited for; matrix products, arithmetic and copies ran while one was open for 22% of the time, Pallas kernels for 0%

commit v1 on v0

v1 whole, which is shorter than its diff:
```python
from functools import partial

import jax
import jax.numpy as jnp
from jax import lax
from jax.experimental import pallas as pl
from jax.experimental.pallas import tpu as pltpu
from jax.sharding import Mesh
from jax.sharding import PartitionSpec as P

DK = 128
DV = 256
CH = 128
EPS_NORM = 1e-06
EPS_GATE = 1e-05
FLOAT = jnp.float32
HALF = jnp.bfloat16
NN = (((1,), (0,)), ((), ()))
NT = (((1,), (1,)), ((), ()))
TN = (((0,), (0,)), ((), ()))
LIMIT = 48 * 1024 * 1024


def mm(a, b, dims=NN):
    return lax.dot_general(a.astype(HALF), b.astype(HALF), dims, preferred_element_type=FLOAT)


def halves(a):
    high = a.astype(HALF)
    return high, (a - high.astype(FLOAT)).astype(HALF)


def mm2(a, b, dims=NN):
    high, low = halves(b)
    return mm(a, high, dims) + mm(a, low, dims)


def mm3(a, b, dims=NN):
    a_high, a_low = halves(a)
    b_high, b_low = halves(b)
    return mm(a_high, b_high, dims) + (mm(a_high, b_low, dims) + mm(a_low, b_high, dims))


def sigmoid(v):
    return 1.0 / (1.0 + jnp.exp(-v))


def square_masks():
    rows = lax.broadcasted_iota(jnp.int32, (CH, CH), 0)
    cols = lax.broadcasted_iota(jnp.int32, (CH, CH), 1)
    return rows, cols


def decay_matrix(gcol, grow):
    rows, cols = square_masks()
    return jnp.where(rows >= cols, jnp.exp(jnp.minimum(gcol - grow, 0.0)), 0.0)


def conv_of(wide, taps, start, count, lanes):
    total = wide[5 + start : 5 + start + count, lanes] * taps[0:1, lanes]
    for j in range(1, 4):
        total = total + wide[5 + j + start : 5 + j + start + count, lanes] * taps[j : j + 1, lanes]
    return total


def prepare_kernel(heads, chunks, proj, taps, betas, gcol, grow, q_out, k_out, v_out, t_out, n_out, b_out, w_out, u_out, p_out, pay, wide):
    rows, cols = square_masks()
    differ = rows ^ cols
    eye = jnp.where(rows == cols, 1.0, 0.0)
    wide[...] = proj[...].astype(FLOAT)
    kq = heads * DK
    work = [(h, c) for h in range(heads) for c in range(chunks)]
    low, keys, sides = {}, {}, {}
    for h, c in work:
        span = slice(c * CH, (c + 1) * CH)
        ql, kl, vl = (
            slice(h * DK, (h + 1) * DK),
            slice(kq + h * DK, kq + (h + 1) * DK),
            slice(2 * kq + h * DV, 2 * kq + (h + 1) * DV),
        )
        cq = conv_of(wide, taps, c * CH, CH, ql)
        query = (cq * sigmoid(cq)).astype(HALF)
        ck = conv_of(wide, taps, c * CH, CH, kl)
        act = ck * sigmoid(ck)
        key = (act * lax.rsqrt(jnp.sum(act * act, axis=-1, keepdims=True) + EPS_NORM)).astype(HALF)
        cv = conv_of(wide, taps, c * CH, CH, vl)
        value = (cv * sigmoid(cv)).astype(HALF)
        q_out[span, ql] = query
        k_out[span, ql] = key
        v_out[span, h * DV : (h + 1) * DV] = value
        beta = betas[span, h : h + 1]
        g = gcol[span, h : h + 1]
        spread = decay_matrix(g, grow[h * chunks + c : h * chunks + c + 1, :])
        inner = mm(key, key, NT)
        low[h, c] = jnp.where(rows > cols, beta * spread * inner, 0.0)
        p_out[h * chunks + c] = (spread * mm(query, key, NT)).astype(HALF)
        keys[h, c] = key
        sides[h, c] = jnp.concatenate([(beta * jnp.exp(g)) * key.astype(FLOAT), beta * value.astype(FLOAT)], axis=1)
    tri = {at: eye - jnp.where(differ < 2, low[at], 0.0) for at in work}
    size = 2
    while size < CH:
        part = {at: mm3(jnp.where((differ >= size) & (differ < 2 * size), low[at], 0.0), tri[at]) for at in work}
        tri = {at: tri[at] - mm3(tri[at], part[at]) for at in work}
        size *= 2
    steps = {}
    for h, c in work:
        at = h * chunks + c
        t_out[at] = tri[h, c].astype(HALF)
        solved = mm3(tri[h, c], sides[h, c])
        w_out[at] = solved[:, :DK].astype(HALF)
        u_out[at] = solved[:, DK:].astype(HALF)
        g = gcol[c * CH : (c + 1) * CH, h : h + 1]
        last = gcol[(c + 1) * CH - 1 : (c + 1) * CH, h : h + 1]
        step = mm2(keys[h, c], jnp.exp(last - g) * solved, TN)
        n_out[at] = step[:, :DK].astype(HALF)
        b_out[at] = step[:, DK:]
        steps[h, c] = (jnp.exp(last), step)
    zero = jnp.zeros((DK, DK), FLOAT)
    for h in range(heads):
        decay, step = steps[h, 0]
        total = jnp.concatenate([decay * eye - step[:, :DK], step[:, DK:]], axis=1)
        whole = decay
        for c in range(1, chunks):
            decay, step = steps[h, c]
            total = decay * total - mm3(step[:, :DK], total) + jnp.concatenate([zero, step[:, DK:]], axis=1)
            whole = whole * decay
        pack_map(pay, h, total, whole, eye)


def whole_decay(pay, j, h):
    return pay[j, h, DK : DK + 1, 0:1].astype(FLOAT) + pay[j, h, DK + 8 : DK + 9, 0:1].astype(FLOAT)


def apply_whole(pay, j, h, state, dims):
    return whole_decay(pay, j, h) * state + mm(pay[j, h, :DK, :DK], state, dims)


def pack_map(pay, h, total, whole, eye):
    pay[h, :DK, :] = jnp.concatenate([total[:, :DK] - whole * eye, total[:, DK:]], axis=1).astype(HALF)
    rest = jnp.broadcast_to(whole, (8, DK + DV))
    first = rest.astype(HALF).astype(FLOAT)
    pay[h, DK:, :] = jnp.concatenate([first, rest - first], axis=0).astype(HALF)


def group_kernel(heads, mine, near, before, group):
    me = mine[0]
    rows, cols = square_masks()
    eye = jnp.where(rows == cols, 1.0, 0.0)
    zero = jnp.zeros((DK, DK), FLOAT)
    start = jnp.concatenate([eye, jnp.zeros((DK, DV), FLOAT)], axis=1)
    totals, keeps, wholes = [start] * heads, [start] * heads, [jnp.ones((1, 1), FLOAT)] * heads
    for j in range(near.shape[0]):
        for h in range(heads):
            added = jnp.concatenate([zero, near[j, h, :DK, DK:].astype(FLOAT)], axis=1)
            if j == 0:
                moved = jnp.concatenate([whole_decay(near, j, h) * eye + near[j, h, :DK, :DK].astype(FLOAT), added[:, DK:]], axis=1)
            else:
                moved = apply_whole(near, j, h, totals[h], NN) + added
            totals[h] = moved
            wholes[h] = wholes[h] * whole_decay(near, j, h)
            keeps[h] = jnp.where(me == j + 1, moved, keeps[h])
    for h in range(heads):
        before[h] = keeps[h]
        pack_map(group, h, totals[h], wholes[h], eye)


def group_back_kernel(heads, mine, near, ends, after, group):
    me = mine[0]
    rows, cols = square_masks()
    eye = jnp.where(rows == cols, 1.0, 0.0)
    zero = jnp.zeros((DK, DK), FLOAT)
    start = jnp.concatenate([eye, jnp.zeros((DK, DV), FLOAT)], axis=1)
    totals, keeps = [start] * heads, [start] * heads
    for j in reversed(range(near.shape[0])):
        for h in range(heads):
            keeps[h] = jnp.where(me == j, totals[h], keeps[h])
            added = jnp.concatenate([zero, ends[j, h].astype(FLOAT)], axis=1)
            totals[h] = apply_whole(near, j, h, totals[h], TN) + added
    for h in range(heads):
        after[h] = keeps[h]
        group[h] = totals[h][:, DK:].astype(HALF)


def mix_kernel(heads, chunks, mine, pay, before, q, k, w, u, p, n, b, gcol, gate, gain, s_out, vn_out, o_out, gated):
    ranks = pay.shape[0]
    me = mine[0]
    states = [jnp.zeros((DK, DV), FLOAT) for h in range(heads)]
    for j in range(ranks - 1):
        passed = j < me
        for h in range(heads):
            moved = apply_whole(pay, j, h, states[h], NN) + pay[j, h, :DK, DK:].astype(FLOAT)
            states[h] = jnp.where(passed, moved, states[h])
    for h in range(heads):
        states[h] = mm3(before[h, :, :DK], states[h]) + before[h, :, DK:]
    for c in range(chunks):
        span = slice(c * CH, (c + 1) * CH)
        for h in range(heads):
            at = h * chunks + c
            state = states[h].astype(HALF)
            s_out[at] = state
            g = gcol[span, h : h + 1]
            last = gcol[(c + 1) * CH - 1 : (c + 1) * CH, h : h + 1]
            vn = (u[at].astype(FLOAT) - mm(w[at], state)).astype(HALF)
            vn_out[at] = vn
            out = jnp.exp(g) * mm(q[span, h * DK : (h + 1) * DK], state) + mm(p[at], vn)
            vl = slice(h * DV, (h + 1) * DV)
            o_out[span, vl] = out
            factor = lax.rsqrt(jnp.mean(out * out, axis=-1, keepdims=True) + EPS_GATE)
            pre = gate[span, vl]
            gated[span, vl] = (out * factor * gain[:, vl] * (pre * sigmoid(pre))).astype(HALF)
            if c + 1 < chunks:
                states[h] = jnp.exp(last) * states[h] - mm(n[at], state) + b[at]


def gate_back_kernel(heads, chunks, d_gated, out, gate, gain, q, w, p, n, gcol, do_out, dvn_out, e_out, dpre_out, dgain_out, sums_out, pay):
    dgain = [jnp.zeros((1, DV), FLOAT) for h in range(heads)]
    ends = [None] * heads
    for c in reversed(range(chunks)):
        span = slice(c * CH, (c + 1) * CH)
        for h in range(heads):
            at = h * chunks + c
            vl = slice(h * DV, (h + 1) * DV)
            dg, o, pre, gn = d_gated[span, vl], out[span, vl], gate[span, vl], gain[:, vl]
            sig = sigmoid(pre)
            factor = lax.rsqrt(jnp.mean(o * o, axis=-1, keepdims=True) + EPS_GATE)
            m = o * factor
            s = pre * sig
            dgm = dg * m
            dgain[h] = dgain[h] + jnp.sum(dgm * s, axis=0, keepdims=True)
            dpre = dgm * gn * (sig * (1.0 + pre * (1.0 - sig)))
            dpre_out[span, vl] = dpre.astype(HALF)
            row_sum = jnp.sum(dpre * pre, axis=-1, keepdims=True)
            sums_out[span, :] = row_sum if h == 0 else sums_out[span, :] + row_sum
            e = dg * gn * s
            dout = factor * (e - m * jnp.mean(e * m, axis=-1, keepdims=True))
            do_out[span, vl] = dout.astype(HALF)
            g = gcol[span, h : h + 1]
            last = gcol[(c + 1) * CH - 1 : (c + 1) * CH, h : h + 1]
            dvn = mm(p[at], dout, TN)
            dvn_out[at] = dvn
            source = mm(q[span, h * DK : (h + 1) * DK], jnp.exp(g) * dout, TN) - mm(w[at], dvn, TN)
            e_out[at] = source
            if ends[h] is None:
                ends[h] = source
            else:
                ends[h] = jnp.exp(last) * ends[h] - mm(n[at], ends[h], TN) + source
    for h in range(heads):
        pay[h] = ends[h].astype(HALF)
        dgain_out[0:1, h * DV : (h + 1) * DV] = dgain[h]


def back_kernel(heads, chunks, mine, pay, late, after, q, k, v, betas, gcol, grow, tri, states, vns, dos, dvns, es, ns, proj, taps, dproj_out, halo_out, dlogit_out, dtaps_out, rowsum_out, wide, dconv):
    ranks = pay.shape[0]
    tokens = chunks * CH
    me = mine[0]
    kq = heads * DK
    width = 2 * kq + heads * DV
    rows, cols = square_masks()
    grads = [jnp.zeros((DK, DV), FLOAT) for h in range(heads)]
    for j in reversed(range(1, ranks)):
        passed = j > me
        for h in range(heads):
            moved = apply_whole(pay, j, h, grads[h], TN) + late[j, h].astype(FLOAT)
            grads[h] = jnp.where(passed, moved, grads[h])
    for h in range(heads):
        grads[h] = mm3(after[h, :, :DK], grads[h]) + after[h, :, DK:]
    wide[...] = proj[...].astype(FLOAT)
    dconv[0:8, :] = jnp.zeros((8, width), FLOAT)
    dconv[8 + tokens :, :] = jnp.zeros((8, width), FLOAT)
    for c in reversed(range(chunks)):
        span = slice(c * CH, (c + 1) * CH)
        for h in range(heads):
            at = h * chunks + c
            ql, kl, vl, ol = (
                slice(h * DK, (h + 1) * DK),
                slice(kq + h * DK, kq + (h + 1) * DK),
                slice(2 * kq + h * DV, 2 * kq + (h + 1) * DV),
                slice(h * DV, (h + 1) * DV),
            )
            grad = grads[h].astype(HALF)
            query, key, value = q[span, ql], k[span, ql], v[span, ol]
            state, vn, dout = states[at], vns[at], dos[span, ol]
            beta = betas[span, h : h + 1]
            g = gcol[span, h : h + 1]
            last = gcol[(c + 1) * CH - 1 : (c + 1) * CH, h : h + 1]
            eg, ed = jnp.exp(g), jnp.exp(last - g)
            spread = decay_matrix(g, grow[at : at + 1, :])
            strict = jnp.where(rows > cols, spread, 0.0)
            inner = mm(key, key, NT)
            dvn = dvns[at] + ed * mm(key, grad)
            dr = mm(tri[at], dvn, TN)
            drh = dr.astype(HALF)
            ks = mm(key, state)
            dval = beta * dr
            both = mm(jnp.concatenate([dout, drh], axis=0), state, NT)
            dkeep = mm(vn, grad, NT)
            pair = mm(jnp.concatenate([dout, drh], axis=0), vn, NT)
            dqk = spread * pair[:CH]
            da = -(strict * pair[CH:])
            dkk = beta * da
            dbeta = jnp.sum(dr * (value.astype(FLOAT) - eg * ks), axis=-1, keepdims=True) + jnp.sum(
                da * inner, axis=-1, keepdims=True
            )
            dqkh = dqk.astype(HALF)
            dkkh = dkk.astype(HALF)
            dquery = eg * both[:CH] + mm(dqkh, key)
            dkey = (
                ed * dkeep
                - (beta * eg) * both[CH:]
                + mm(dqkh, query, TN)
                + mm(dkkh, key)
                + mm(dkkh, key, TN)
            )
            if c > 0:
                grads[h] = jnp.exp(last) * grads[h] - mm(ns[at], grad, TN) + es[at]
            dlogit_out[span, h : h + 1] = dbeta * beta * (1.0 - beta)
            there = slice(8 + c * CH, 8 + (c + 1) * CH)
            cq = conv_of(wide, taps, c * CH, CH, ql)
            sig = sigmoid(cq)
            dconv[there, ql] = dquery * (sig * (1.0 + cq * (1.0 - sig)))
            cv = conv_of(wide, taps, c * CH, CH, vl)
            sig = sigmoid(cv)
            dconv[there, vl] = dval * (sig * (1.0 + cv * (1.0 - sig)))
            ck = conv_of(wide, taps, c * CH, CH, kl)
            sig = sigmoid(ck)
            act = ck * sig
            unit = lax.rsqrt(jnp.sum(act * act, axis=-1, keepdims=True) + EPS_NORM)
            u = act * unit
            dact = unit * (dkey - u * jnp.sum(dkey * u, axis=-1, keepdims=True))
            dconv[there, kl] = dact * (sig * (1.0 + ck * (1.0 - sig)))
    dtaps_out[4:8, :] = jnp.zeros((4, width), FLOAT)
    rowsum_out[...] = jnp.zeros((8 + tokens, 1), FLOAT)
    for at in range(0, width, DK):
        lanes = slice(at, at + DK)
        for j in range(4):
            dtaps_out[j : j + 1, lanes] = jnp.sum(
                dconv[8 : 8 + tokens, lanes] * wide[5 + j : 5 + j + tokens, lanes], axis=0, keepdims=True
            )
        total = dconv[3 : 3 + 8 + tokens, lanes] * taps[0:1, lanes]
        for j in range(1, 4):
            total = total + dconv[3 - j : 3 - j + 8 + tokens, lanes] * taps[j : j + 1, lanes]
        halo_out[:, lanes] = total[0:8]
        small = total.astype(HALF)
        dproj_out[:, lanes] = small
        rowsum_out[...] += jnp.sum(small.astype(FLOAT) * wide[:, lanes], axis=-1, keepdims=True)


def out(shape, dtype):
    return jax.ShapeDtypeStruct(shape, dtype)


def run(kernel, shapes, args, scratch=(), scalars=0):
    vmem = pl.BlockSpec(memory_space=pltpu.VMEM)
    smem = pl.BlockSpec(memory_space=pltpu.SMEM)
    return pl.pallas_call(
        kernel,
        out_shape=shapes,
        in_specs=[smem] * scalars + [vmem] * (len(args) - scalars),
        out_specs=[vmem] * len(shapes),
        scratch_shapes=list(scratch),
        compiler_params=pltpu.CompilerParams(vmem_limit_bytes=LIMIT),
    )(*args)


def prepare_shapes(heads, chunks):
    tokens, pairs = chunks * CH, heads * chunks
    return (
        out((tokens, heads * DK), HALF),
        out((tokens, heads * DK), HALF),
        out((tokens, heads * DV), HALF),
        out((pairs, CH, CH), HALF),
        out((pairs, DK, DK), HALF),
        out((pairs, DK, DV), FLOAT),
        out((pairs, CH, DK), HALF),
        out((pairs, CH, DV), HALF),
        out((pairs, CH, CH), HALF),
        out((heads, DK + 16, DK + DV), HALF),
    )


def mix_shapes(heads, chunks):
    tokens, pairs = chunks * CH, heads * chunks
    return (
        out((pairs, DK, DV), HALF),
        out((pairs, CH, DV), HALF),
        out((tokens, heads * DV), FLOAT),
        out((tokens, heads * DV), HALF),
    )


def gate_back_shapes(heads, chunks):
    tokens, pairs = chunks * CH, heads * chunks
    return (
        out((tokens, heads * DV), HALF),
        out((pairs, CH, DV), FLOAT),
        out((pairs, DK, DV), FLOAT),
        out((tokens, heads * DV), HALF),
        out((1, heads * DV), FLOAT),
        out((tokens, 1), FLOAT),
        out((heads, DK, DV), HALF),
    )


def back_shapes(heads, chunks):
    tokens = chunks * CH
    width = heads * (2 * DK + DV)
    return (
        out((8 + tokens, width), HALF),
        out((8, width), FLOAT),
        out((tokens, heads), FLOAT),
        out((8, width), FLOAT),
        out((8 + tokens, 1), FLOAT),
    )


def back_scratch(heads, chunks):
    tokens = chunks * CH
    width = heads * (2 * DK + DV)
    return (pltpu.VMEM((8 + tokens, width), FLOAT), pltpu.VMEM((16 + tokens, width), FLOAT))


def group_shapes(heads):
    return (out((heads, DK, DK + DV), FLOAT), out((heads, DK + 16, DK + DV), HALF))


def group_back_shapes(heads):
    return (out((heads, DK, DK + DV), FLOAT), out((heads, DK, DV), HALF))


HEAD = ("x", "c")
SEQ = ("y", "z")
CONTRACT_ROWS = (((0,), (0,)), ((), ()))
CONTRACT_COLS = (((1,), (1,)), ((), ()))


def rotated(array, axis, distance):
    size = lax.axis_size(axis)
    return lax.ppermute(array, axis, [(i, (i + distance) % size) for i in range(size)])


def ring_gather(array, axis):
    mine = lax.axis_index(axis)
    size = lax.axis_size(axis)
    arrived = [(rotated(array, axis, d), -d) for d in (1, -1, 2)]
    whole = jnp.zeros((size, *array.shape), array.dtype)
    for piece, offset in [(array, 0), *arrived]:
        whole = lax.dynamic_update_index_in_dim(whole, piece, (mine + offset) % size, 0)
    return whole


def head_gather(array):
    core = lax.axis_index("c")
    whole = ring_gather(array, "x")
    other = rotated(whole, "c", 1)
    both = jnp.where(core == 0, jnp.stack([whole, other], 1), jnp.stack([other, whole], 1))
    return both.reshape(8, *array.shape)


def head_scatter(tiles):
    mine, core = lax.axis_index("x"), lax.axis_index("c")
    tiles = tiles.reshape(4, 2, *tiles.shape[1:])
    own = lax.dynamic_index_in_dim(tiles, core, 1, False)
    other = rotated(lax.dynamic_index_in_dim(tiles, 1 - core, 1, False), "c", 1)
    summed = (own.astype(FLOAT) + other.astype(FLOAT)).astype(HALF)
    total = lax.dynamic_index_in_dim(summed, mine, 0, False).astype(FLOAT)
    for d in (1, -1, 2):
        sent = lax.dynamic_index_in_dim(summed, (mine + d) % 4, 0, False)
        total = total + rotated(sent, "x", d).astype(FLOAT)
    return total


def next_block(array, distance):
    size = 16
    route = [(i, i + distance) for i in range(size) if 0 <= i + distance < size]
    return lax.ppermute(array, SEQ, route)


def dot(a, b):
    return jnp.dot(a, b, preferred_element_type=FLOAT)


def dot_nt(a, b):
    return lax.dot_general(a, b, CONTRACT_COLS, preferred_element_type=FLOAT)


def dot_tn(a, b):
    return lax.dot_general(a, b, CONTRACT_ROWS, preferred_element_type=FLOAT)


def silu_grad(v):
    s = jax.nn.sigmoid(v)
    return s * (1.0 + v * (1.0 - s))


def seq_scatter(array):
    return lax.psum_scatter(array.astype(HALF), SEQ, scatter_dimension=0, tiled=True).astype(FLOAT)


def side_by_side(blocks):
    count, rows, cols = blocks.shape
    return blocks.transpose(1, 0, 2).reshape(rows, count * cols)


def shards(
    block_input,
    log_decay,
    first_gain,
    query_weight,
    key_weight,
    value_weight,
    gate_weight,
    beta_weight,
    query_conv,
    key_conv,
    value_conv,
    mixer_gain,
    mixer_weight,
    second_gain,
    swiglu_gate,
    swiglu_up,
    swiglu_down,
    cotangent,
):
    heads = log_decay.shape[1]
    tokens, width = block_input.shape
    chunks = tokens // CH
    rows = tokens // 8
    kq = heads * DK
    rank = lax.axis_index("x") * 2 + lax.axis_index("c")
    z_rank = lax.axis_index("z").astype(jnp.int32).reshape(1)
    y_rank = lax.axis_index("y").astype(jnp.int32).reshape(1)

    in_weight = jnp.concatenate([query_weight, key_weight, value_weight], axis=1)
    taps = jnp.concatenate([query_conv, key_conv, value_conv], axis=0).T
    gcol = jnp.cumsum(log_decay.reshape(chunks, CH, heads), axis=1)
    grow = gcol.transpose(2, 0, 1).reshape(heads * chunks, CH)
    gcol = gcol.reshape(tokens, heads)
    gain_row = mixer_gain.reshape(1, -1)

    halo = next_block(block_input[tokens - 8 :], 1)
    whole = side_by_side(head_gather(block_input))
    whole = jnp.concatenate([side_by_side(head_gather(halo)), whole], axis=0).astype(FLOAT)
    first_factor = lax.rsqrt(jnp.mean(whole * whole, axis=-1, keepdims=True) + EPS_NORM)
    first_normed = (whole * first_factor * first_gain).astype(HALF)
    proj = dot(first_normed, in_weight).astype(HALF)
    logits = dot(first_normed[8:], beta_weight)
    betas = jax.nn.sigmoid(logits)
    gate_pre = dot(first_normed[8:], gate_weight)
    q, k, v, tri, n, b, w, u, p, pay = run(
        partial(prepare_kernel, heads, chunks),
        prepare_shapes(heads, chunks),
        (proj, taps, betas, gcol, grow),
        [pltpu.VMEM((8 + tokens, taps.shape[1]), FLOAT)],
    )
    near = ring_gather(pay, "z")
    before, group = run(
        partial(group_kernel, heads), group_shapes(heads), (z_rank, near), scalars=1
    )
    far = ring_gather(group, "y")
    states, vns, mixed, gated = run(
        partial(mix_kernel, heads, chunks),
        mix_shapes(heads, chunks),
        (y_rank, far, before, q, k, w, u, p, n, b, gcol, gate_pre, gain_row),
        scalars=1,
    )
    branch = head_scatter(dot_nt(gated, mixer_weight).astype(HALF).reshape(8, rows, -1))
    my_rows = lax.dynamic_slice_in_dim(whole, 8 + rank * rows, rows, 0)
    hidden = my_rows + branch
    second_factor = lax.rsqrt(jnp.mean(hidden * hidden, axis=-1, keepdims=True) + EPS_NORM)
    second_unit = hidden * second_factor
    second_normed = head_gather((second_unit * second_gain).astype(HALF)).reshape(tokens, -1)
    gate_act = dot(second_normed, swiglu_gate)
    up_act = dot(second_normed, swiglu_up)
    silu_act = jax.nn.silu(gate_act)
    product = (silu_act * up_act).astype(HALF)
    whole_cot = side_by_side(head_gather(cotangent))
    d_product = dot(whole_cot, swiglu_down)
    d_gate = (d_product * up_act * silu_grad(gate_act)).astype(HALF)
    d_up = (d_product * silu_act).astype(HALF)
    d_second = head_scatter(
        (dot_nt(d_gate, swiglu_gate) + dot_nt(d_up, swiglu_up)).astype(HALF).reshape(8, rows, -1)
    )
    grad_swiglu_down = seq_scatter(dot_tn(whole_cot, product))
    grad_swiglu_gate = seq_scatter(dot_tn(second_normed, d_gate))
    grad_swiglu_up = seq_scatter(dot_tn(second_normed, d_up))
    second_gain_part = jnp.sum(d_second * second_unit, axis=0)
    e = d_second * second_gain
    cot_rows = lax.dynamic_slice_in_dim(whole_cot, rank * rows, rows, 0).astype(FLOAT)
    d_hidden = cot_rows + second_factor * (
        e - second_unit * jnp.mean(e * second_unit, axis=-1, keepdims=True)
    )
    d_branch = head_gather(d_hidden.astype(HALF)).reshape(tokens, -1)
    d_gated = dot(d_branch, mixer_weight)
    dos, dvns, es, d_gate_pre, gain_part, gate_sums, ends = run(
        partial(gate_back_kernel, heads, chunks),
        gate_back_shapes(heads, chunks),
        (d_gated, mixed, gate_pre, gain_row, q, w, p, n, gcol),
    )
    near_ends = ring_gather(ends, "z")
    after, group_end = run(
        partial(group_back_kernel, heads), group_back_shapes(heads), (z_rank, near, near_ends), scalars=1
    )
    far_ends = ring_gather(group_end, "y")
    grad_mixer_weight = seq_scatter(dot_tn(d_branch, gated))
    grad_gate_weight = seq_scatter(dot_tn(first_normed[8:], d_gate_pre))
    d_first_part = dot_nt(d_gate_pre, gate_weight)
    dproj, halo_grad, d_logit, taps_part, sums = run(
        partial(back_kernel, heads, chunks),
        back_shapes(heads, chunks),
        (y_rank, far, far_ends, after, q, k, v, betas, gcol, grow, tri, states, vns, dos, dvns, es, n, proj, taps),
        back_scratch(heads, chunks),
        scalars=1,
    )
    grad_in_weight = seq_scatter(dot_tn(first_normed, dproj))
    grad_beta = dot_tn(first_normed[8:], d_logit.astype(HALF))
    arrived = next_block(halo_grad, -1)
    last = dproj[tokens:].astype(FLOAT) + arrived
    d_own = jnp.concatenate([dproj[8:tokens], last.astype(HALF)], axis=0)
    late_sums = jnp.sum(arrived * proj[tokens:].astype(FLOAT), axis=-1)
    row_sums = sums[8:, 0] + gate_sums[:, 0] + jnp.sum(d_logit * logits, axis=-1)
    row_sums = row_sums + jnp.concatenate([jnp.zeros((tokens - 8,), FLOAT), late_sums])
    d_first_part = d_first_part + dot_nt(d_own, in_weight)
    d_first_part = d_first_part + dot_nt(d_logit.astype(HALF), beta_weight)
    in_blocks = d_first_part.astype(HALF).reshape(tokens, 8, width).transpose(1, 0, 2)
    d_first = head_scatter(in_blocks)
    row_mean = lax.psum(row_sums, HEAD) / (8 * width)
    own_input = block_input.astype(FLOAT)
    own_factor = first_factor[8:]
    own_unit = own_input * own_factor
    own_gain = lax.dynamic_slice_in_dim(first_gain, rank * width, width, 0)
    d_branch_own = lax.dynamic_slice_in_dim(d_branch, rank * width, width, 1).astype(FLOAT)
    grad_input = d_branch_own + own_factor * (d_first * own_gain - own_unit * row_mean[:, None])
    first_gain_part = lax.dynamic_update_slice_in_dim(
        jnp.zeros((8 * width,), FLOAT), jnp.sum(d_first * own_unit, axis=0), rank * width, 0
    )
    down_part = dot_nt(product, swiglu_down)
    mine = lax.dynamic_slice_in_dim(down_part, rank * rows, rows, 0) + hidden
    down_part = lax.dynamic_update_slice_in_dim(down_part, mine, rank * rows, 0)
    output = head_scatter(down_part.astype(HALF).reshape(tokens, 8, width).transpose(1, 0, 2)).astype(HALF)
    small = [taps_part[:4], gain_part, grad_beta]
    ends_at = [0]
    for part in small:
        ends_at.append(ends_at[-1] + part.size)
    flat = lax.psum(jnp.concatenate([part.ravel() for part in small]), SEQ)
    taps_grad, grad_mixer_gain, grad_beta = (
        flat[at:to].reshape(part.shape) for part, at, to in zip(small, ends_at, ends_at[1:])
    )
    gains = lax.psum(jnp.stack([first_gain_part, second_gain_part]), SEQ + HEAD)
    seq_rank = lax.axis_index("y") * 4 + lax.axis_index("z")
    share = 8 * width // 16
    gains = lax.dynamic_slice_in_dim(gains, seq_rank * share, share, 1)
    grad_beta = lax.dynamic_slice_in_dim(grad_beta, seq_rank * share, share, 0)
    return (
        output,
        grad_input,
        gains[0],
        grad_in_weight[:, :kq],
        grad_in_weight[:, kq : 2 * kq],
        grad_in_weight[:, 2 * kq :],
        grad_gate_weight,
        grad_beta,
        taps_grad[:, :kq].T,
        taps_grad[:, kq : 2 * kq].T,
        taps_grad[:, 2 * kq :].T,
        grad_mixer_gain[0],
        grad_mixer_weight,
        gains[1],
        grad_swiglu_gate,
        grad_swiglu_up,
        grad_swiglu_down,
    )


def solution(mesh):
    torus = Mesh(mesh.devices.reshape(4, 4, 4, 2), SEQ + HEAD)
    in_specs = (
        P(SEQ, HEAD),
        P(SEQ, HEAD),
        P(),
        P(None, HEAD),
        P(None, HEAD),
        P(None, HEAD),
        P(None, HEAD),
        P(None, HEAD),
        P(HEAD, None),
        P(HEAD, None),
        P(HEAD, None),
        P(HEAD),
        P(None, HEAD),
        P(),
        P(None, HEAD),
        P(None, HEAD),
        P(None, HEAD),
        P(SEQ, HEAD),
    )
    out_specs = (
        P(SEQ, HEAD),
        P(SEQ, HEAD),
        P(SEQ),
        P(SEQ, HEAD),
        P(SEQ, HEAD),
        P(SEQ, HEAD),
        P(SEQ, HEAD),
        P(SEQ, HEAD),
        P(HEAD, None),
        P(HEAD, None),
        P(HEAD, None),
        P(HEAD),
        P(SEQ, HEAD),
        P(SEQ),
        P(SEQ, HEAD),
        P(SEQ, HEAD),
        P(SEQ, HEAD),
    )
    return jax.shard_map(
        shards, mesh=torus, in_specs=in_specs, out_specs=out_specs, check_vma=False
    )
```

time: 1180 us -> 647 us (0.55)
  matrix products: 398 us -> 65.3 us
  local copies, waits for them, and re-layouts: 227 us -> 65.8 us
  other arithmetic: 168 us -> 29.1 us
  blocking collectives: 87 us -> 157 us
  starting transfers between devices: 32.2 us -> 63.7 us
  Pallas kernels: 0 us -> 28.8 us
  waiting for transfers between devices: 239 us -> 217 us
    dot_general x261 -> x21, matrix products: 389 us -> 65.3 us  [the longest x7 25.2 us: dot_nt(): return lax.dot_general(a, b, CONTRACT_COLS, preferred_element_type=FLOAT)]
    psum x0 -> x3, blocking collectives: none -> 157 us  [the longest x1 74.6 us: shards(): flat = lax.psum(jnp.concatenate([part.ravel() for part in small]), SEQ)]
    psum x3 -> x0, waiting for transfers between devices: 121 us -> none  [the longest x1 54 us: shards(): lax.psum(d_second_part.astype(jnp.bfloat16), 'head').astype(jnp.float32)]
    reduce_scatter x0 -> x3, waiting for transfers between devices: none -> 119 us  [seq_scatter(): lax.psum_scatter(array.astype(HALF), SEQ, scatter_dimension=0, tiled=True)]
    all_gather x6 -> x0, blocking collectives: 87 us -> none  [the longest x4 53.3 us: prefix_by_axis_2(): lax.all_gather(part.astype(kind), axis)]
    ppermute x2 -> x50, waiting for transfers between devices: 11.2 us -> 97.9 us  [the longest x48 97.9 us: rotated(): lax.ppermute(array, axis, [(i, (i + distance) % size) for i in range(size)])]
    another operation x8 -> x2, other arithmetic: 81.8 us -> 0.28 us  [the longest x1 0.26 us: shards(): gcol = jnp.cumsum(log_decay.reshape(chunks, CH, heads), axis=1)]
    ppermute x2 -> x50, starting transfers between devices: 6.49 us -> 62.8 us  [the longest x48 57.4 us: rotated(): lax.ppermute(array, axis, [(i, (i + distance) % size) for i in range(size)])]
  transfers between devices with their start and end apart: 13 -> 56, of which waited for: 10 -> 31; matrix products, arithmetic and copies ran while one was open for 22% -> 18% of each run, Pallas kernels for 0% -> 2%
where the time goes in v1:
time: 647 us; the launch traced here: 642 us
  waiting for transfers between devices  217 us (34%)
  blocking collectives  157 us (24%)
  local copies, waits for them, and re-layouts  65.8 us (10%)
  matrix products  65.3 us (10%)
  starting transfers between devices  63.7 us (10%)
  other arithmetic  29.1 us (4%)
  Pallas kernels  28.8 us (4%)
  between operations  16 us (2%)
    reduce_scatter x3, waiting for transfers between devices, seq_scatter(): lax.psum_scatter(array.astype(HALF), SEQ, scatter_dimension=0, tiled=True)  119 us
    ppermute x48, waiting for transfers between devices, rotated(): lax.ppermute(array, axis, [(i, (i + distance) % size) for i in range(size)])  97.9 us
    psum x1, blocking collectives, shards(): flat = lax.psum(jnp.concatenate([part.ravel() for part in small]), SEQ)  74.6 us
    psum x1, blocking collectives, shards(): gains = lax.psum(jnp.stack([first_gain_part, second_gain_part]), SEQ + HEAD)  63.5 us
    ppermute x48, starting transfers between devices, rotated(): lax.ppermute(array, axis, [(i, (i + distance) % size) for i in range(size)])  57.4 us
    unnamed x165, local copies, waits for them, and re-layouts  37.6 us
    pallas_call x6, Pallas kernels, run(): pl.pallas_call(kernel, out_shape=shapes, in_specs=[smem] * scalars + [vme...  28.8 us
    dot_general x7, matrix products, dot_nt(): return lax.dot_general(a, b, CONTRACT_COLS, preferred_element_type=FLOAT)  25.2 us
  transfers between devices with their start and end apart: 56, of which 31 were waited for; matrix products, arithmetic and copies ran while one was open for 18% of the time, Pallas kernels for 2%

profile of v1, /device:TPU:2, one launch (start us, length us, event | category | flops | bytes accessed | tf_op | source)
XLA Modules:
  0.0 642.1 jit_solution(8829775977154996429)
XLA Ops:
  12.2 3.9 collective-permute-start
  42.1 8.2 %shard_map.305 = (bf16[512,256]{1,0:T(8,128)(2,1)S(1)}, bf16[512,256]{1,0:T(8,128)(2,1)S(1)}, bf16[512,512]{1,0:T(8,128)(2,1)S(1)}, bf16[8,128,128]{2,1,0:T(8,12...) custom-call(bf16[520,1024]{1,0:T(8,128)(2,1)S(1)} %convolution_conve, ...), custom_call_target="tpu_custom_call" | custom-call | tf_op jit(solution)/shard_map/pallas_call | solution.py:355
  62.2 3.8 collective-permute-done.11
  76.0 3.8 collective-permute-done.13
  81.8 4.2 shard_map.307
  95.2 9.5 %collective-permute-done.27 = bf16[512,256]{1,0:T(8,128)(2,1)} collective-permute-done((bf16[512,256]{1,0:T(8,128)(2,1)}, bf16[512,256]{1,0:T(8,128)(2,1)}, u32[]{:S(2)}, u32[]{:S(2)}) %collective-permute-start.27) | collective-permute-done | bytes 262176 | tf_op jit(solution)/shard_map/ppermute | solution.py:438
  112.3 9.0 %collective-permute-done.16 = bf16[64,2048]{1,0:T(8,128)(2,1)S(1)} collective-permute-done((bf16[64,2048]{1,0:T(8,128)(2,1)S(1)}, bf16[64,2048]{1,0:T(8,128)(2,1)S(1)}, u32[]{:S(2)}, u32[]{:S(2)}) %collective-permute-start.16) | collective-permute-done | bytes 262176 | tf_op jit(solution)/shard_map/ppermute | solution.py:438
  131.0 4.5 collective-permute-done.20
  135.5 6.8 %collective-permute-done.21 = bf16[64,2048]{1,0:T(8,128)(2,1)S(1)} collective-permute-done((bf16[64,2048]{1,0:T(8,128)(2,1)S(1)}, bf16[64,2048]{1,0:T(8,128)(2,1)S(1)}, u32[]{:S(2)}, u32[]{:S(2)}) %collective-permute-start.21) | collective-permute-done | bytes 262176 | tf_op jit(solution)/shard_map/ppermute | solution.py:438
  151.7 3.5 multiply_convert_fusion.1
  156.1 3.3 convolution_convert_fusion.3
  159.5 4.6 copy.131
  164.1 5.1 convolution_convert_fusion.2
  169.3 4.7 copy.133
  194.6 4.0 fusion.34
  199.8 6.8 %collective-permute-done.34 = bf16[64,2048]{1,0:T(8,128)(2,1)S(1)} collective-permute-done((bf16[64,2048]{1,0:T(8,128)(2,1)S(1)}, bf16[64,2048]{1,0:T(8,128)(2,1)S(1)}, u32[]{:S(2)}, u32[]{:S(2)}) %collective-permute-start.34) | collective-permute-done | bytes 262176 | tf_op jit(solution)/shard_map/ppermute | solution.py:438
  213.8 5.7 collective-permute-done.35
  219.6 5.1 collective-permute-done.37
  232.3 3.5 fusion.37.d_gated
  235.8 3.6 shard_map.308
  259.0 6.1 collective-permute-done.42
  266.2 11.5 %shard_map.310 = (bf16[520,1024]{1,0:T(8,128)(2,1)}, f32[8,1024]{1,0:T(8,128)S(1)}, f32[512,2]{1,0:T(8,128)S(1)}, f32[8,1024]{1,0:T(8,128)S(1)}, f32[520,1]{1,0:T(8,128)S(1)}) custom-call(s32[1]{0:T(128)} %bitcast.19.mine, bf16[4,2,144,384]{3,2,1,0:T(8,128)(2,1)S(1)} %copy-done.5, bf16[4,2,128,256]{3,2,1,0:T(8,128)(2,1)S(1)} %bitcast_dynamic-update-slice_fusion.24.late, ...), custom_call_target="tpu_custom_call" | custom-call | tf_op jit(solution)/shard_map/pallas_call | solution.py:355
  277.7 6.3 convolution_convert_fusion
  294.3 3.9 collective-permute-start.26
  302.8 6.8 %collective-permute-done.26 = bf16[512,256]{1,0:T(8,128)(2,1)S(1)} collective-permute-done((bf16[512,256]{1,0:T(8,128)(2,1)S(1)}, bf16[512,256]{1,0:T(8,128)(2,1)S(1)}, u32[]{:S(2)}, u32[]{:S(2)}) %collective-permute-start.26) | collective-permute-done | bytes 262176 | tf_op jit(solution)/shard_map/ppermute | solution.py:438
  311.4 5.1 fusion.38
  324.1 74.6 %psum.23 = f32[8704]{0:T(1024)S(1)} all-reduce(f32[8704]{0:T(1024)S(1)} %pad_maximum_fusion), channel_id=1, replica_groups=mesh['y'=4,'z'=4,'x'=4,'c'=2] {'y','z'}, use_global_device_ids=true, to_apply=%region_12.13 | all-reduce | flops 8704 | bytes 69632 | tf_op jit(solution)/shard_map/psum | solution.py:644
  400.2 7.1 %add_convert_fusion = bf16[512,2048]{1,0:T(8,128)(2,1)S(1)} fusion(f32[512,2048]{1,0:T(8,128)} %fusion.26, f32[512,2048]{1,0:T(8,128)} %fusion.38, bf16[2048,1024]{1,0:T(8,128)(2,1)} %copy-done.63, bf16[8,1024]{1,0:T(8,128)(2,1)S(1)} %get-tuple-element.176, bf16[504,1024]{1,0:T(8,128)(2,1)S(1)} %slice.74), kind=kOutput, calls=%fused_computation.2 | convolution fusion | flops 2152726528 | bytes 15728640 | tf_op jit(solution)/shard_map/dot_general | solution.py:483
  419.3 18.8 %psum.21 = f32[512]{0:T(512)S(1)} all-reduce(f32[512]{0:T(512)S(1)} %pad_add_fusion), channel_id=1, replica_groups=mesh['y'=4,'z'=4,'x'=4,'c'=2] {'x','c'}, use_global_device_ids=true, to_apply=%region_6.7 | all-reduce | flops 512 | bytes 4096 | tf_op jit(solution)/shard_map/psum | solution.py:626
  440.2 63.5 %psum.22 = f32[2,2048]{1,0:T(2,128)S(1)} all-reduce(f32[2,2048]{1,0:T(2,128)S(1)} %pad_maximum_fusion.2), channel_id=1, replica_groups=mesh['y'=4,'z'=4,'x'=4,'c'=2] {'y','z','x','c'}, use_global_device_ids=true, to_apply=%region_9.10 | all-reduce | flops 4096 | bytes 32768 | tf_op jit(solution)/shard_map/psum | solution.py:648
  511.6 40.1 %reduce-scatter.15.cloned.1.call-done = bf16[128,512]{1,0:T(8,128)(2,1)} async-done(((bf16[2048,512]{1,0:T(8,128)(2,1)}), bf16[128,512]{1,0:T(8,128)(2,1)}) %reduce-scatter.15.cloned.1.call-update) | async-done | bytes 131088 | tf_op jit(solution)/shard_map/reduce_scatter | solution.py:496
  553.3 78.5 %reduce-scatter.13.cloned.1.call-done = bf16[128,1024]{1,0:T(8,128)(2,1)} async-done(((bf16[2048,1024]{1,0:T(8,128)(2,1)}), bf16[128,1024]{1,0:T(8,128)(2,1)}) %reduce-scatter.13.cloned.1.call-update) | async-done | bytes 262160 | tf_op jit(solution)/shard_map/reduce_scatter | solution.py:496
  (395 shorter events, 200.3 us)
Async XLA Ops:
  7.2 497.0 %reduce-scatter.19.cloned.1.call-start = ((), (), s32[]{:S(2)}) async-start(), calls=%async_computation.9 | async-start | bytes 3342336
  7.3 16.6 %collective-permute-start.5 = (bf16[512,256]{1,0:T(8,128)(2,1)}, bf16[512,256]{1,0:T(8,128)(2,1)}, u32[]{:S(2)}, u32[]{:S(2)}) collective-permute-start(bf16[512,256]{1,0:T(8,128)(2,1)} %param.18), channel_id=1, source_target_pairs={{0,2},{2,4},{4,6},{6,0},{1,3},{3,5},{5,7},{7,1},{8,10},{10,12},{12... | collective-permute-start | bytes 786440 | tf_op jit(solution)/shard_map/ppermute | solution.py:438
  8.8 18.3 %collective-permute-start.6 = (bf16[512,256]{1,0:T(8,128)(2,1)}, bf16[512,256]{1,0:T(8,128)(2,1)}, u32[]{:S(2)}, u32[]{:S(2)}) collective-permute-start(bf16[512,256]{1,0:T(8,128)(2,1)} %param.18), channel_id=1, source_target_pairs={{0,6},{2,0},{4,2},{6,4},{1,7},{3,1},{5,3},{7,5},{8,14},{10,8},{12,... | collective-permute-start | bytes 786440 | tf_op jit(solution)/shard_map/ppermute | solution.py:438
  9.4 19.4 %collective-permute-start.7 = (bf16[512,256]{1,0:T(8,128)(2,1)}, bf16[512,256]{1,0:T(8,128)(2,1)S(1)}, u32[]{:S(2)}, u32[]{:S(2)}) collective-permute-start(bf16[512,256]{1,0:T(8,128)(2,1)} %param.18), channel_id=1, source_target_pairs={{0,4},{2,6},{4,0},{6,2},{1,5},{3,7},{5,1},{7,3},{8,12},{10,14},{12... | collective-permute-start | bytes 786440 | tf_op jit(solution)/shard_map/ppermute | solution.py:438
  12.2 9.7 %collective-permute-start = (bf16[8,256]{1,0:T(8,128)(2,1)S(1)}, bf16[8,256]{1,0:T(8,128)(2,1)S(1)}, u32[]{:S(2)}, u32[]{:S(2)}) collective-permute-start(bf16[8,256]{1,0:T(8,128)(2,1)S(1)} %slice.71), channel_id=1, source_target_pairs={{0,8},{8,16},{16,24},{24,32},{32,40},{40,48},{48,56},{56,64},{64,7... | collective-permute-start | bytes 12296 | tf_op jit(solution)/shard_map/ppermute | solution.py:475
  55.1 10.8 %collective-permute-start.11 = (bf16[2,144,384]{2,1,0:T(8,128)(2,1)S(1)}, bf16[2,144,384]{2,1,0:T(8,128)(2,1)S(1)}, u32[]{:S(2)}, u32[]{:S(2)}) collective-permute-start(bf16[2,144,384]{2,1,0:T(8,128)(2,1)S(1)} %get-tuple-element.47), channel_id=1, source_target_pairs={{0,16},{8,24},{16,0},{24,8},{1,17},{9,25},{17,1},{25,9},{2,18},{10... | collective-permute-start | bytes 663560 | tf_op jit(solution)/shard_map/ppermute | solution.py:438
  69.1 10.7 %collective-permute-start.13 = (bf16[2,144,384]{2,1,0:T(8,128)(2,1)S(1)}, bf16[2,144,384]{2,1,0:T(8,128)(2,1)S(1)}, u32[]{:S(2)}, u32[]{:S(2)}) collective-permute-start(bf16[2,144,384]{2,1,0:T(8,128)(2,1)S(1)} %get-tuple-element.48), channel_id=1, source_target_pairs={{0,96},{32,0},{64,32},{96,64},{1,97},{33,1},{65,33},{97,65},{2,98}... | collective-permute-start | bytes 663560 | tf_op jit(solution)/shard_map/ppermute | solution.py:438
  70.8 10.9 %collective-permute-start.14 = (bf16[2,144,384]{2,1,0:T(8,128)(2,1)S(1)}, bf16[2,144,384]{2,1,0:T(8,128)(2,1)S(1)}, u32[]{:S(2)}, u32[]{:S(2)}) collective-permute-start(bf16[2,144,384]{2,1,0:T(8,128)(2,1)S(1)} %get-tuple-element.48), channel_id=1, source_target_pairs={{0,64},{32,96},{64,0},{96,32},{1,65},{33,97},{65,1},{97,33},{2,66}... | collective-permute-start | bytes 663560 | tf_op jit(solution)/shard_map/ppermute | solution.py:438
  89.9 15.8 %collective-permute-start.15 = (bf16[4,64,2048]{2,1,0:T(8,128)(2,1)}, bf16[4,64,2048]{2,1,0:T(8,128)(2,1)}, u32[]{:S(2)}, u32[]{:S(2)}) collective-permute-start(bf16[4,64,2048]{2,1,0:T(8,128)(2,1)} %dynamic-slice_bitcast_fusion.3), channel_id=1, source_target_pairs={{0,1},{1,0},{2,3},{3,2},{4,5},{5,4},{6,7},{7,6},{8,9},{9,8},{10,11... | collective-permute-start | bytes 3145736 | tf_op jit(solution)/shard_map/ppermute | solution.py:438
  89.9 14.8 %collective-permute-start.27 = (bf16[512,256]{1,0:T(8,128)(2,1)}, bf16[512,256]{1,0:T(8,128)(2,1)}, u32[]{:S(2)}, u32[]{:S(2)}) collective-permute-start(bf16[512,256]{1,0:T(8,128)(2,1)} %param.35), channel_id=1, source_target_pairs={{0,2},{2,4},{4,6},{6,0},{1,3},{3,5},{5,7},{7,1},{8,10},{10,12},{12... | collective-permute-start | bytes 786440 | tf_op jit(solution)/shard_map/ppermute | solution.py:438
  92.6 31.8 %collective-permute-start.28 = (bf16[512,256]{1,0:T(8,128)(2,1)}, bf16[512,256]{1,0:T(8,128)(2,1)}, u32[]{:S(2)}, u32[]{:S(2)}) collective-permute-start(bf16[512,256]{1,0:T(8,128)(2,1)} %param.35), channel_id=1, source_target_pairs={{0,6},{2,0},{4,2},{6,4},{1,7},{3,1},{5,3},{7,5},{8,14},{10,8},{12,... | collective-permute-start | bytes 786440 | tf_op jit(solution)/shard_map/ppermute | solution.py:438
  92.6 32.7 %collective-permute-start.29 = (bf16[512,256]{1,0:T(8,128)(2,1)}, bf16[512,256]{1,0:T(8,128)(2,1)}, u32[]{:S(2)}, u32[]{:S(2)}) collective-permute-start(bf16[512,256]{1,0:T(8,128)(2,1)} %param.35), channel_id=1, source_target_pairs={{0,4},{2,6},{4,0},{6,2},{1,5},{3,7},{5,1},{7,3},{8,12},{10,14},{12... | collective-permute-start | bytes 786440 | tf_op jit(solution)/shard_map/ppermute | solution.py:438
  107.6 13.6 %collective-permute-start.16 = (bf16[64,2048]{1,0:T(8,128)(2,1)S(1)}, bf16[64,2048]{1,0:T(8,128)(2,1)S(1)}, u32[]{:S(2)}, u32[]{:S(2)}) collective-permute-start(bf16[64,2048]{1,0:T(8,128)(2,1)S(1)} %get-tuple-element.168), channel_id=1, source_target_pairs={{0,2},{2,4},{4,6},{6,0},{1,3},{3,5},{5,7},{7,1},{8,10},{10,12},{12... | collective-permute-start | bytes 786440 | tf_op jit(solution)/shard_map/ppermute | solution.py:438
  110.2 13.3 %collective-permute-start.17 = (bf16[64,2048]{1,0:T(8,128)(2,1)S(1)}, bf16[64,2048]{1,0:T(8,128)(2,1)S(1)}, u32[]{:S(2)}, u32[]{:S(2)}) collective-permute-start(bf16[64,2048]{1,0:T(8,128)(2,1)S(1)} %get-tuple-element.170), channel_id=1, source_target_pairs={{0,6},{2,0},{4,2},{6,4},{1,7},{3,1},{5,3},{7,5},{8,14},{10,8},{12,... | collective-permute-start | bytes 786440 | tf_op jit(solution)/shard_map/ppermute | solution.py:438
  110.2 13.3 %collective-permute-start.18 = (bf16[64,2048]{1,0:T(8,128)(2,1)S(1)}, bf16[64,2048]{1,0:T(8,128)(2,1)S(1)}, u32[]{:S(2)}, u32[]{:S(2)}) collective-permute-start(bf16[64,2048]{1,0:T(8,128)(2,1)S(1)} %get-tuple-element.169), channel_id=1, source_target_pairs={{0,4},{2,6},{4,0},{6,2},{1,5},{3,7},{5,1},{7,3},{8,12},{10,14},{12... | collective-permute-start | bytes 786440 | tf_op jit(solution)/shard_map/ppermute | solution.py:438
  126.3 16.3 %collective-permute-start.30 = (bf16[4,512,256]{2,1,0:T(8,128)(2,1)S(1)}, bf16[4,512,256]{2,1,0:T(8,128)(2,1)S(1)}, u32[]{:S(2)}, u32[]{:S(2)}) collective-permute-start(bf16[4,512,256]{2,1,0:T(8,128)(2,1)S(1)} %bitcast_dynamic-update-slice_fusion.4), channel_id=1, source_target_pairs={{0,1},{1,0},{2,3},{3,2},{4,5},{5,4},{6,7},{7,6},{8,9},{9,8},{10,11... | collective-permute-start | bytes 3145736 | tf_op jit(solution)/shard_map/ppermute | solution.py:438
  128.2 14.0 %collective-permute-start.21 = (bf16[64,2048]{1,0:T(8,128)(2,1)S(1)}, bf16[64,2048]{1,0:T(8,128)(2,1)S(1)}, u32[]{:S(2)}, u32[]{:S(2)}) collective-permute-start(bf16[64,2048]{1,0:T(8,128)(2,1)S(1)} %get-tuple-element.151), channel_id=1, source_target_pairs={{0,4},{2,6},{4,0},{6,2},{1,5},{3,7},{5,1},{7,3},{8,12},{10,14},{12... | collective-permute-start | bytes 786440 | tf_op jit(solution)/shard_map/ppermute | solution.py:438
  164.1 342.1 %reduce-scatter.21.cloned.1.call-start = ((), (), s32[]{:S(2)}) async-start(), calls=%async_computation.10 | async-start | bytes 3342336
  174.0 334.1 %reduce-scatter.23.cloned.1.call-start = ((), (), s32[]{:S(2)}) async-start(), calls=%async_computation.11 | async-start | bytes 3342336
  187.0 322.9 %reduce-scatter.17.cloned.1.call-start = ((), (), s32[]{:S(2)}) async-start(), calls=%async_computation.8 | async-start | bytes 2228224 | tf_op jit(solution)/shard_map/reduce_scatter | solution.py:496
  190.5 9.4 %collective-permute-start.33 = (bf16[64,2048]{1,0:T(8,128)(2,1)S(1)}, bf16[64,2048]{1,0:T(8,128)(2,1)S(1)}, u32[]{:S(2)}, u32[]{:S(2)}) collective-permute-start(bf16[64,2048]{1,0:T(8,128)(2,1)S(1)} %get-tuple-element.164), channel_id=1, source_target_pairs={{0,6},{2,0},{4,2},{6,4},{1,7},{3,1},{5,3},{7,5},{8,14},{10,8},{12,... | collective-permute-start | bytes 786440 | tf_op jit(solution)/shard_map/ppermute | solution.py:438
  192.5 14.2 %collective-permute-start.34 = (bf16[64,2048]{1,0:T(8,128)(2,1)S(1)}, bf16[64,2048]{1,0:T(8,128)(2,1)S(1)}, u32[]{:S(2)}, u32[]{:S(2)}) collective-permute-start(bf16[64,2048]{1,0:T(8,128)(2,1)S(1)} %get-tuple-element.163), channel_id=1, source_target_pairs={{0,4},{2,6},{4,0},{6,2},{1,5},{3,7},{5,1},{7,3},{8,12},{10,14},{12... | collective-permute-start | bytes 786440 | tf_op jit(solution)/shard_map/ppermute | solution.py:438
  212.3 12.4 %collective-permute-start.37 = (bf16[64,2048]{1,0:T(8,128)(2,1)S(1)}, bf16[64,2048]{1,0:T(8,128)(2,1)S(1)}, u32[]{:S(2)}, u32[]{:S(2)}) collective-permute-start(bf16[64,2048]{1,0:T(8,128)(2,1)S(1)} %get-tuple-element.148), channel_id=1, source_target_pairs={{0,4},{2,6},{4,0},{6,2},{1,5},{3,7},{5,1},{7,3},{8,12},{10,14},{12... | collective-permute-start | bytes 786440 | tf_op jit(solution)/shard_map/ppermute | solution.py:438
  232.1 319.6 %reduce-scatter.15.cloned.1.call-start = ((), (), s32[]{:S(2)}) async-start(), calls=%async_computation.7 | async-start | bytes 2228224 | tf_op jit(solution)/shard_map/reduce_scatter | solution.py:496
  244.5 387.2 %reduce-scatter.13.cloned.1.call-start = ((), (), s32[]{:S(2)}) async-start(), calls=%async_computation.6 | async-start | bytes 4456448 | tf_op jit(solution)/shard_map/reduce_scatter | solution.py:496
  255.6 9.5 %collective-permute-start.42 = (bf16[2,128,256]{2,1,0:T(8,128)(2,1)S(1)}, bf16[2,128,256]{2,1,0:T(8,128)(2,1)S(1)}, u32[]{:S(2)}, u32[]{:S(2)}) collective-permute-start(bf16[2,128,256]{2,1,0:T(8,128)(2,1)S(1)} %get-tuple-element.61), channel_id=1, source_target_pairs={{0,32},{32,64},{64,96},{96,0},{1,33},{33,65},{65,97},{97,1},{2,34}... | collective-permute-start | bytes 393224 | tf_op jit(solution)/shard_map/ppermute | solution.py:438
  293.1 9.7 %collective-permute-start.25 = (bf16[512,256]{1,0:T(8,128)(2,1)S(1)}, bf16[512,256]{1,0:T(8,128)(2,1)S(1)}, u32[]{:S(2)}, u32[]{:S(2)}) collective-permute-start(bf16[512,256]{1,0:T(8,128)(2,1)S(1)} %get-tuple-element.167), channel_id=1, source_target_pairs={{0,6},{2,0},{4,2},{6,4},{1,7},{3,1},{5,3},{7,5},{8,14},{10,8},{12,... | collective-permute-start | bytes 786440 | tf_op jit(solution)/shard_map/ppermute | solution.py:438
  294.3 15.3 %collective-permute-start.26 = (bf16[512,256]{1,0:T(8,128)(2,1)S(1)}, bf16[512,256]{1,0:T(8,128)(2,1)S(1)}, u32[]{:S(2)}, u32[]{:S(2)}) collective-permute-start(bf16[512,256]{1,0:T(8,128)(2,1)S(1)} %get-tuple-element.166), channel_id=1, source_target_pairs={{0,4},{2,6},{4,0},{6,2},{1,5},{3,7},{5,1},{7,3},{8,12},{10,14},{12... | collective-permute-start | bytes 786440 | tf_op jit(solution)/shard_map/ppermute | solution.py:438
  320.0 79.4 %collective-permute-start.45 = (f32[8,1024]{1,0:T(8,128)S(1)}, f32[8,1024]{1,0:T(8,128)S(1)}, u32[]{:S(2)}, u32[]{:S(2)}) collective-permute-start(f32[8,1024]{1,0:T(8,128)S(1)} %get-tuple-element.71), channel_id=1, source_target_pairs={{8,0},{16,8},{24,16},{32,24},{40,32},{48,40},{56,48},{64,56},{72,6... | collective-permute-start | bytes 98312 | tf_op jit(solution)/shard_map/ppermute | solution.py:475
  415.3 22.7 %collective-permute-start.47 = (bf16[512,256]{1,0:T(8,128)(2,1)S(1)}, bf16[512,256]{1,0:T(8,128)(2,1)S(1)}, u32[]{:S(2)}, u32[]{:S(2)}) collective-permute-start(bf16[512,256]{1,0:T(8,128)(2,1)S(1)} %get-tuple-element.159), channel_id=1, source_target_pairs={{0,2},{2,4},{4,6},{6,0},{1,3},{3,5},{5,7},{7,1},{8,10},{10,12},{12... | collective-permute-start | bytes 786440 | tf_op jit(solution)/shard_map/ppermute | solution.py:438
  415.4 22.6 %collective-permute-start.48 = (bf16[512,256]{1,0:T(8,128)(2,1)S(1)}, bf16[512,256]{1,0:T(8,128)(2,1)S(1)}, u32[]{:S(2)}, u32[]{:S(2)}) collective-permute-start(bf16[512,256]{1,0:T(8,128)(2,1)S(1)} %get-tuple-element.161), channel_id=1, source_target_pairs={{0,6},{2,0},{4,2},{6,4},{1,7},{3,1},{5,3},{7,5},{8,14},{10,8},{12,... | collective-permute-start | bytes 786440 | tf_op jit(solution)/shard_map/ppermute | solution.py:438
  417.4 20.6 %collective-permute-start.49 = (bf16[512,256]{1,0:T(8,128)(2,1)S(1)}, bf16[512,256]{1,0:T(8,128)(2,1)S(1)}, u32[]{:S(2)}, u32[]{:S(2)}) collective-permute-start(bf16[512,256]{1,0:T(8,128)(2,1)S(1)} %get-tuple-element.160), channel_id=1, source_target_pairs={{0,4},{2,6},{4,0},{6,2},{1,5},{3,7},{5,1},{7,3},{8,12},{10,14},{12... | collective-permute-start | bytes 786440 | tf_op jit(solution)/shard_map/ppermute | solution.py:438
  (101 other events, 1062.2 us)
Sparse Core Ops, SparseCore 0:
  164.2 74.6 reduce-scatter.18
  242.3 76.9 reduce-scatter.20
  322.6 74.9 reduce-scatter.22
  400.8 73.6 reduce-scatter.16
  477.9 73.6 reduce-scatter.14
  554.8 76.9 reduce-scatter.12
